TPU v7x, 128 devices: a whole 4x4x4 slice. The times are simulated.
128 devices in a mesh: seq: 16 (over x_hi, y, core), chan: 8 (over z, x_lo).
Axes of the slice: x: 4 (x_hi: 2, x_lo: 2; x = x_hi * 2 + x_lo), y: 4, z: 4, core: 2. Of those that a mesh axis runs over, the one named last changes fastest.
Arguments:
- residual_in: bfloat16 [4096, 4096], P('seq', 'chan')
- mr_query: bfloat16 [4096, 4096], P('seq', 'chan'), may hold values from -6 to 6
- mr_key: bfloat16 [4096, 4096], P('seq', 'chan'), may hold values from -6 to 6
- mr_value: bfloat16 [4096, 4096], P('seq', 'chan'), may hold values from -6 to 6
- mr_short: bfloat16 [3, 3, 4096], P(None, None, 'chan'), may hold values from -3.5 to 3.5
- mr_filter: bfloat16 [128, 4096], P(None, 'chan'), may hold values from -0.5 to 0.5
- mix_weight: bfloat16 [4096, 4096], P('chan'), may hold values from -0.125 to 0.125
- norm_gain: bfloat16 [4096], P('chan'), may hold values from 0.099609375 to 1.8984375
- li_weight: bfloat16 [3, 4096, 4096], P(None, None, 'chan'), may hold values from -0.09375 to 0.09375
- li_short: bfloat16 [3, 3, 4096], P(None, None, 'chan'), may hold values from -3.5 to 3.5
- li_rate: float32 [4096, 16], P('chan'), as said below
- li_residue: float32 [4096, 16], P('chan')
- decode_slot: int32 [128], P('chan'), may hold values from 0 to 127, as said below
Outputs:
- li_out: bfloat16 [4096, 4096], P('seq', 'chan')
- residual_out: bfloat16 [4096, 4096], P('seq', 'chan')
- decode_state: float32 [128, 512], P(('seq', 'chan'))
Inputs may be any that keep to these rules, and one draw needn't show every extreme that they name: `decode_slot`: the 128 slots are distinct; the slot q of block b satisfies (q) % 8 == b // 16. `li_rate`: positive decay rates.
All inputs are finite; a program needn't handle non-finite values.
Results may differ from a plain program's by a relative error of at most 0.035.
Values may be sent and summed in bfloat16 or wider, within the bound.
A program may use at most 320 MiB of HBM per device.

v0:
```python
import jax
import jax.numpy as jnp
from jax import lax
from jax.sharding import PartitionSpec as P

D = 4096
MODES = 16
CB = 32
BLK = 128


EPSILON = 1e-06
HIGHEST_PRECISION = lax.Precision.HIGHEST


def from_behind(shard, axis, by):
    length = lax.axis_size(axis)
    pairs = [(i, i + by) for i in range(length) if 0 <= i + by < length]
    return lax.ppermute(shard, axis, pairs)


def entering_2(shard, axis, combine, identity):
    length, here = (lax.axis_size(axis), lax.axis_index(axis))
    everything = jax.tree.map(
        lambda part, kind: lax.all_gather(part.astype(kind), axis),
        shard,
        (jnp.bfloat16, jnp.bfloat16),
    )
    start = jax.tree.map(
        lambda part, zero: jnp.broadcast_to(jnp.asarray(zero, part.dtype), part.shape),
        shard,
        identity,
    )

    def hop(k, before):
        reached = k < here
        new = combine(
            before, jax.tree.map(lambda part, own: part[k].astype(own.dtype), everything, shard)
        )
        return jax.tree.map(lambda a, b: jnp.where(reached, a, b), new, before)

    return lax.fori_loop(0, length, hop, start)


def for_sending(shard):
    return jax.tree.map(lambda a: a.astype(jnp.bfloat16) if a.dtype == jnp.float32 else a, shard)


def broadcast(block, axis, source):
    block = jnp.where(lax.axis_index(axis) == source, block, jnp.zeros_like(block))
    return lax.psum(block, axis)


def short_filter(extended, taps_weight, short_lead):
    out_rows = extended.shape[0] - short_lead
    running = jnp.zeros((out_rows, extended.shape[1]), jnp.float32)
    for offset in range(taps_weight.shape[0]):
        window = extended[short_lead - offset : short_lead - offset + out_rows]
        running = running + taps_weight[offset].astype(jnp.float32)[None, :] * window.astype(
            jnp.float32
        )
    return running


def short_three(extended, taps_weight, short_lead, chan_width):
    query_short = short_filter(extended[:, :chan_width], taps_weight[0], short_lead)
    key_short = short_filter(extended[:, chan_width : 2 * chan_width], taps_weight[1], short_lead)
    value_short = short_filter(extended[:, 2 * chan_width :], taps_weight[2], short_lead)
    return (query_short, key_short, value_short)


def toeplitz_rows(period_rows, row_count, col_count):
    period = period_rows.shape[0]
    tiled = jnp.tile(period_rows, (row_count, 1))
    shaped = tiled[: row_count * (period - 1)].reshape(row_count, period - 1, period_rows.shape[1])
    return shaped[:, :col_count]


def tap_conv(extended, filter_taps, block_size):
    out_rows = extended.shape[0] - block_size
    block_count = out_rows // block_size
    tap_count = filter_taps.shape[0]
    chan_width = filter_taps.shape[1]
    earlier = extended[:out_rows].reshape(block_count, block_size, -1)
    current = extended[block_size:].reshape(block_count, block_size, -1)
    joined = jnp.concatenate([earlier, current], axis=1)
    period_rows = jnp.concatenate(
        [
            jnp.zeros((block_size - tap_count + 1, chan_width), filter_taps.dtype),
            filter_taps[::-1],
            jnp.zeros((2 * block_size - 1, chan_width), filter_taps.dtype),
        ],
        axis=0,
    )
    matrix = toeplitz_rows(period_rows, block_size, 2 * block_size)
    result = jnp.einsum("tsc,bsc->btc", matrix, joined, preferred_element_type=jnp.float32)
    return result.reshape(out_rows, -1)


def modal_tables(rate_part, residue_part, block_size):
    offsets = jnp.arange(block_size, dtype=jnp.float32)
    kernel = jnp.sum(
        residue_part[None] * jnp.exp(-rate_part[None] * offsets[:, None, None]), axis=2
    )
    chan_width = kernel.shape[1]
    period_rows = jnp.concatenate(
        [kernel[:1], jnp.zeros((block_size, chan_width), jnp.float32), kernel[1:][::-1]], axis=0
    )
    lower_band = toeplitz_rows(period_rows, block_size, block_size)
    end_weights = jnp.exp(-rate_part[None] * (block_size - 1.0 - offsets)[:, None, None])
    start_weights = residue_part[None] * jnp.exp(-rate_part[None] * (offsets + 1.0)[:, None, None])
    step_decay = jnp.exp(-rate_part * block_size)
    return (lower_band, end_weights, start_weights, step_decay)


def modal_sweep(block_states, start_state, step_decay):

    def advance(carried, block_state):
        return (step_decay * carried + block_state, carried)

    leaving, entering = lax.scan(advance, start_state, block_states)
    return (leaving, entering)


def link_spans(earlier, later):
    return (earlier[0] * later[0], later[0] * earlier[1] + later[1])


def local(
    residual_in,
    mr_query,
    mr_key,
    mr_value,
    mr_short,
    mr_filter,
    mix_weight,
    norm_gain,
    li_weight,
    li_short,
    li_rate,
    li_residue,
    decode_slot,
):
    local_rows, chan_width = mr_query.shape
    short_lead = mr_short.shape[1] - 1
    tap_count = mr_filter.shape[0]
    joined = jnp.concatenate([mr_query, mr_key, mr_value], axis=1)
    border = from_behind(joined[local_rows - short_lead :], "seq", 1)
    extended = jnp.concatenate([border, joined], axis=0)
    query_short, key_short, value_short = short_three(extended, mr_short, short_lead, chan_width)
    mr_input = (key_short * value_short).astype(jnp.bfloat16)
    input_rim = from_behind(mr_input[local_rows - (tap_count - 1) :], "seq", 1)
    padded = jnp.concatenate(
        [jnp.zeros((BLK - (tap_count - 1), chan_width), jnp.bfloat16), input_rim, mr_input], axis=0
    )
    mr_conv = tap_conv(padded, mr_filter, BLK)
    mr_gated = (query_short * mr_conv).astype(jnp.bfloat16)
    partial_value = jnp.dot(mr_gated, mix_weight, preferred_element_type=jnp.float32)
    mixed = lax.psum_scatter(
        partial_value.astype(jnp.bfloat16), "chan", scatter_dimension=1, tiled=True
    ).astype(jnp.float32)
    residual_sum = residual_in.astype(jnp.float32) + mixed
    squares = lax.psum(jnp.sum(residual_sum * residual_sum, axis=1), "chan")
    inverse = lax.rsqrt(squares[:, None] / D + EPSILON)
    normed = (residual_sum * inverse * norm_gain.astype(jnp.float32)[None, :]).astype(jnp.bfloat16)
    projected = jnp.einsum(
        "tk,ikc->itc",
        lax.all_gather(normed, "chan", axis=1, tiled=True),
        li_weight,
        preferred_element_type=jnp.float32,
    )
    residual_out = residual_sum.astype(jnp.bfloat16)
    li_proj = projected.astype(jnp.bfloat16)
    li_border = from_behind(li_proj[:, local_rows - short_lead :, :], "seq", 1)
    li_extended = jnp.concatenate([li_border, li_proj], axis=1)
    li_query = short_filter(li_extended[0], li_short[0], short_lead)
    li_key = short_filter(li_extended[1], li_short[1], short_lead)
    li_value = short_filter(li_extended[2], li_short[2], short_lead)
    li_input = (li_key * li_value).astype(jnp.bfloat16)
    block_count = local_rows // BLK
    input_blocks = li_input.astype(jnp.float32).reshape(block_count, BLK, chan_width)
    lower_band, end_weights, start_weights, step_decay = modal_tables(li_rate, li_residue, BLK)
    within = jnp.einsum("tsc,bsc->btc", lower_band, input_blocks, precision=HIGHEST_PRECISION)
    block_states = jnp.einsum(
        "tcm,btc->bcm", end_weights, input_blocks, precision=HIGHEST_PRECISION
    )
    zero_state = jnp.zeros((chan_width, MODES), jnp.float32)
    own_end, entering = modal_sweep(block_states, zero_state, step_decay)
    device_decay = jnp.exp(-li_rate * local_rows)
    identity = (jnp.ones((chan_width, MODES), jnp.float32), zero_state)
    prefix = entering_2((device_decay, own_end), "seq", link_spans, identity)
    incoming = prefix[1]
    final_state = device_decay * incoming + own_end
    blocks = (li_residue * final_state).reshape(chan_width // CB, CB * MODES)
    blocks = broadcast(for_sending(blocks), "seq", lax.axis_size("seq") - 1).astype(blocks.dtype)
    powers = jnp.exp(
        -li_rate[None] * BLK * jnp.arange(block_count, dtype=jnp.float32)[:, None, None]
    )
    entering = entering + powers * incoming[None]
    across = jnp.einsum("tcm,bcm->btc", start_weights, entering, precision=HIGHEST_PRECISION)
    li_conv = (within + across).reshape(local_rows, chan_width)
    li_out = (li_query * li_conv).astype(jnp.bfloat16)
    own_count = blocks.shape[0] // lax.axis_size("seq")
    my_slots = (
        lax.axis_index("seq") * lax.axis_size("chan") + lax.axis_index("chan")
    ) * own_count + jnp.arange(own_count)
    chooser = (decode_slot[None, :] == my_slots[:, None]).astype(jnp.float32)
    decode_local = jnp.dot(chooser, blocks, precision=HIGHEST_PRECISION)
    return (li_out, residual_out, decode_local)


def solution(mesh):
    in_specs = (
        P("seq", "chan"),
        P("seq", "chan"),
        P("seq", "chan"),
        P("seq", "chan"),
        P(None, None, "chan"),
        P(None, "chan"),
        P("chan", None),
        P("chan"),
        P(None, None, "chan"),
        P(None, None, "chan"),
        P("chan", None),
        P("chan", None),
        P("chan"),
    )
    out_specs = (P("seq", "chan"), P("seq", "chan"), P(("seq", "chan"), None))
    return jax.shard_map(local, mesh=mesh, in_specs=in_specs, out_specs=out_specs, check_vma=False)
```

profile of v0, /device:TPU:1, one launch (start us, length us, event | category | flops | bytes accessed | tf_op | source)
XLA Modules:
  0.0 645.4 jit_solution(1733705186400587828)
XLA Ops:
  10.1 4.6 collective-permute-start
  21.4 16.3 %tile.8 = bf16[128,384,512]{2,1,0:T(8,128)(2,1)} broadcast(bf16[384,512]{1,0:T(8,128)(2,1)S(1)} %maximum_maximum_fusion), dimensions={1,2} | broadcast | bytes 50724864 | tf_op jit(solution)/shard_map/tile | solution.py:74
  37.6 33.6 %slice.269 = bf16[49024,512]{1,0:T(8,128)(2,1)} slice(bf16[49152,512]{1,0:T(8,128)(2,1)} %bitcast.111), slice={[0:49024], [0:512]} | slice | bytes 100401152 | tf_op jit(solution)/shard_map/slice | solution.py:75
  71.2 40.7 %reshape.295 = bf16[128,383,512]{2,1,0:T(8,128)(2,1)} reshape(bf16[49024,512]{1,0:T(8,128)(2,1)} %slice.269) | data formatting | bytes 100401152 | tf_op jit(solution)/shard_map/reshape | solution.py:75
  111.9 22.8 %slice.270 = bf16[128,256,512]{2,1,0:T(8,128)(2,1)} slice(bf16[128,383,512]{2,1,0:T(8,128)(2,1)} %reshape.295), slice={[0:128], [0:256], [0:512]} | slice | bytes 67108864 | tf_op jit(solution)/shard_map/slice | solution.py:76
  134.8 45.6 %copy.93 = bf16[128,256,512]{1,0,2:T(8,128)(2,1)} copy(bf16[128,256,512]{2,1,0:T(8,128)(2,1)} %slice.270) | data formatting | bytes 67108864
  180.8 14.5 %convolution_bitcast_fusion = f32[2,128,512]{1,0,2:T(2,128)S(1)} fusion(bf16[128,256,512]{1,0,2:T(8,128)(2,1)} %copy.93, bf16[2,128,512]{1,0,2:T(2,128)(2,1)S(1)} %copy.91, bf16[2,128,512]{1,0,2:T(2,128)(2,1)S(1)} %copy.90), kind=kOutput, calls=%fused_computation.36 | convolution fusion | flops 68157440 | bytes 34603008 | tf_op jit(solution)/shard_map/tsc,bsc->btc/dot_general | solution.py:96
  195.8 4.8 convolution_convert_fusion
  200.7 56.5 %reduce-scatter.2.cloned.1.call-done = bf16[256,512]{1,0:T(8,128)(2,1)} async-done(((bf16[256,4096]{1,0:T(8,128)(2,1)}), bf16[256,512]{1,0:T(8,128)(2,1)}) %reduce-scatter.2.cloned.1.call-update) | async-done | bytes 262160 | tf_op jit(solution)/shard_map/reduce_scatter | solution.py:159
  258.4 13.1 %psum.14 = f32[256]{0:T(256)S(1)} all-reduce(f32[256]{0:T(256)S(1)} %multiply_reduce_fusion.1), channel_id=1, replica_groups=mesh['seq'=16,'chan'=8] {'chan'}, use_global_device_ids=true, to_apply=%region_2.0 | all-reduce | flops 256 | bytes 2048 | tf_op jit(solution)/shard_map/psum | solution.py:163
  273.6 6.0 multiply_reduce_fusion
  280.5 29.4 %all-gather = bf16[8192,16]{0,1:T(8,128)(2,1)S(1)} all-gather(bf16[512,16]{0,1:T(8,128)(2,1)S(1)} %get-tuple-element.233), channel_id=2, replica_groups=mesh['seq'=16,'chan'=8] {'seq'}, dimensions={0}, use_global_device_ids=true | all-gather | bytes 278528 | tf_op jit(solution)/shard_map/all_gather | solution.py:25
  310.6 18.4 %all-gather.4.cloned.1.call-done = bf16[256,4096]{1,0:T(8,128)(2,1)} async-done(((bf16[256,512]{1,0:T(8,128)(2,1)}), bf16[256,4096]{1,0:T(8,128)(2,1)}) %all-gather.4.cloned.1.call-update) | async-done | bytes 2097168 | tf_op jit(solution)/shard_map/all_gather | solution.py:168
  329.0 8.6 %fusion.18 = bf16[3,256,512]{2,1,0:T(8,128)(2,1)S(1)} fusion(bf16[3,4096,512]{2,1,0:T(8,128)(2,1)} %param.25, bf16[256,4096]{1,0:T(8,128)(2,1)} %all-gather.4.cloned.1.call-done), kind=kOutput, calls=%fused_computation.32 | convolution fusion | flops 3221618688 | bytes 15466496 | tf_op jit(solution)/shard_map/tk,ikc->itc/dot_general | solution.py:166
  340.9 21.5 %tile.20 = f32[128,256,512]{2,1,0:T(8,128)} broadcast(f32[256,512]{1,0:T(8,128)S(1)} %pad_maximum_fusion), dimensions={1,2} | broadcast | bytes 67633152 | tf_op jit(solution)/shard_map/tile | solution.py:74
  362.4 43.8 %slice.287 = f32[32640,512]{1,0:T(8,128)} slice(f32[32768,512]{1,0:T(8,128)} %bitcast.34), slice={[0:32640], [0:512]} | slice | bytes 133693440 | tf_op jit(solution)/shard_map/slice | solution.py:75
  406.2 45.7 %reshape.297 = f32[128,255,512]{2,1,0:T(8,128)} reshape(f32[32640,512]{1,0:T(8,128)} %slice.287) | data formatting | bytes 133693440 | tf_op jit(solution)/shard_map/reshape | solution.py:75
  451.9 23.5 %slice.288 = f32[128,128,512]{2,1,0:T(8,128)} slice(f32[128,255,512]{2,1,0:T(8,128)} %reshape.297), slice={[0:128], [0:128], [0:512]} | slice | bytes 67108864 | tf_op jit(solution)/shard_map/slice | solution.py:76
  475.5 35.5 %copy.94 = f32[128,128,512]{1,0,2:T(8,128)} copy(f32[128,128,512]{2,1,0:T(8,128)} %slice.288) | data formatting | bytes 67108864
  511.6 4.1 fusion.22
  516.1 24.4 %all-gather.1 = bf16[8192,16]{0,1:T(8,128)(2,1)S(1)} all-gather(bf16[512,16]{0,1:T(8,128)(2,1)S(1)} %convert_element_type.411), channel_id=3, replica_groups=mesh['seq'=16,'chan'=8] {'seq'}, dimensions={0}, use_global_device_ids=true | all-gather | bytes 278528 | tf_op jit(solution)/shard_map/all_gather | solution.py:25
  541.5 59.4 %psum.15 = bf16[16,512]{1,0:T(8,128)(2,1)S(1)} all-reduce(bf16[16,512]{1,0:T(8,128)(2,1)S(1)} %select_n.35), channel_id=1, replica_groups=mesh['seq'=16,'chan'=8] {'seq'}, use_global_device_ids=true, to_apply=%region_8.9 | all-reduce | flops 8192 | bytes 32768 | tf_op jit(solution)/shard_map/psum | solution.py:51
  601.2 5.7 fusion.1
  606.9 29.8 %fusion.21 = f32[2,128,512]{1,0,2:T(2,128)S(1)} fusion(f32[512,2,128]{2,1,0:T(2,128)S(1)} %fusion.1, bf16[2,128,512]{1,0,2:T(2,128)(2,1)S(1)} %copy.82, f32[128,128,512]{1,0,2:T(8,128)} %copy.94), kind=kOutput, calls=%fused_computation.34 | convolution fusion | flops 201457664 | bytes 34865152 | tf_op jit(solution)/shard_map/tsc,bsc->btc/dot_general | solution.py:183
  (108 shorter events, 22.9 us)
Async XLA Ops:
  7.2 250.1 %reduce-scatter.2.cloned.1.call-start = ((), (), s32[]{:S(2)}) async-start(), calls=%async_computation.1 | async-start | bytes 2359296 | tf_op jit(solution)/shard_map/reduce_scatter | solution.py:159
  10.1 7.2 %collective-permute-start = (bf16[2,1536]{1,0:T(2,128)(2,1)S(1)}, bf16[2,1536]{1,0:T(2,128)(2,1)S(1)}, u32[]{:S(2)}, u32[]{:S(2)}) collective-permute-start(bf16[2,1536]{1,0:T(2,128)(2,1)S(1)} %slice.256), channel_id=1, source_target_pairs={{0,8},{8,16},{16,24},{24,32},{32,40},{40,48},{48,56},{56,64},{64,7... | collective-permute-start | bytes 18440 | tf_op jit(solution)/shard_map/ppermute | solution.py:19
  15.7 21.9 %copy-start.8 = (bf16[384]{0:T(512)(128)(2,1)}, bf16[384]{0:T(512)(128)(2,1)S(1)}, u32[]{:S(2)}) copy-start(bf16[384]{0:T(512)(128)(2,1)S(1)} %pad.10.clone) | copy-start | bytes 2308
  18.8 161.7 %collective-permute-start.1 = (bf16[127,512]{1,0:T(8,128)(2,1)S(1)}, bf16[127,512]{1,0:T(8,128)(2,1)S(1)}, u32[]{:S(2)}, u32[]{:S(2)}) collective-permute-start(bf16[127,512]{1,0:T(8,128)(2,1)S(1)} %slice.267), channel_id=1, source_target_pairs={{0,8},{8,16},{16,24},{24,32},{32,40},{40,48},{48,56},{56,64},{64,7... | collective-permute-start | bytes 390152 | tf_op jit(solution)/shard_map/ppermute | solution.py:19
  134.8 45.7 %slice-start = ((bf16[384]{0:T(512)(128)(2,1)}), bf16[256]{0:T(256)(128)(2,1)S(1)}, s32[]{:S(2)}) async-start(bf16[384]{0:T(512)(128)(2,1)} %copy-done.8), calls=%async_computation.3 | async-start | bytes 1024 | tf_op jit(solution)/shard_map/slice | solution.py:84
  180.8 14.7 %copy-start = (bf16[256,512]{1,0:T(8,128)(2,1)S(1)}, bf16[256,512]{1,0:T(8,128)(2,1)}, u32[]{:S(2)}) copy-start(bf16[256,512]{1,0:T(8,128)(2,1)} %param.18) | copy-start | bytes 786436
  195.7 4.9 copy-start.9
  195.8 61.5 %copy-start.1 = (bf16[256,512]{1,0:T(8,128)(2,1)S(1)}, bf16[256,512]{1,0:T(8,128)(2,1)}, u32[]{:S(2)}) copy-start(bf16[256,512]{1,0:T(8,128)(2,1)} %param.17) | copy-start | bytes 786436
  195.8 77.6 %copy-start.3 = (f32[512,16]{0,1:T(8,128)S(1)}, f32[512,16]{0,1:T(8,128)}, u32[]{:S(2)}) copy-start(f32[512,16]{0,1:T(8,128)} %param.27) | copy-start | bytes 98308
  200.6 72.9 %copy-start.2 = (f32[512,16]{0,1:T(8,128)S(1)}, f32[512,16]{0,1:T(8,128)}, u32[]{:S(2)}) copy-start(f32[512,16]{0,1:T(8,128)} %param.28) | copy-start | bytes 98308
  200.6 109.2 %copy-start.4 = (bf16[3,3,512]{2,1,0:T(4,128)(2,1)S(1)}, bf16[3,3,512]{2,1,0:T(4,128)(2,1)}, u32[]{:S(2)}) copy-start(bf16[3,3,512]{2,1,0:T(4,128)(2,1)} %param.26) | copy-start | bytes 27652
  200.6 128.3 %all-gather.4.cloned.1.call-start = ((), (), s32[]{:S(2)}) async-start(), calls=%async_computation.2 | async-start | bytes 2359296 | tf_op jit(solution)/shard_map/all_gather | solution.py:168
  337.6 173.3 %collective-permute-start.2 = (bf16[3,2,512]{2,1,0:T(2,128)(2,1)S(1)}, bf16[3,2,512]{2,1,0:T(2,128)(2,1)S(1)}, u32[]{:S(2)}, u32[]{:S(2)}) collective-permute-start(bf16[3,2,512]{2,1,0:T(2,128)(2,1)S(1)} %slice.272), channel_id=1, source_target_pairs={{0,8},{8,16},{16,24},{24,32},{32,40},{40,48},{48,56},{56,64},{64,7... | collective-permute-start | bytes 18440 | tf_op jit(solution)/shard_map/ppermute | solution.py:19
  606.8 30.1 %copy-start.10 = (s32[16]{0:T(128)S(1)}, s32[16]{0:T(128)}, u32[]{:S(2)}) copy-start(s32[16]{0:T(128)} %param.29) | copy-start | bytes 196
  606.8 30.8 %copy-start.5 = (f32[1,1,512]{2,1,0:T(1,128)S(1)}, f32[1,1,512]{2,1,0:T(1,128)}, u32[]{:S(2)}) copy-start(f32[1,1,512]{2,1,0:T(1,128)} %get-tuple-element.236) | copy-start | bytes 6148
  606.9 30.8 %copy-start.6 = (f32[1,1,512]{2,1,0:T(1,128)S(1)}, f32[1,1,512]{2,1,0:T(1,128)}, u32[]{:S(2)}) copy-start(f32[1,1,512]{2,1,0:T(1,128)} %get-tuple-element.241) | copy-start | bytes 6148
  606.9 30.8 %copy-start.7 = (f32[1,1,512]{2,1,0:T(1,128)S(1)}, f32[1,1,512]{2,1,0:T(1,128)}, u32[]{:S(2)}) copy-start(f32[1,1,512]{2,1,0:T(1,128)} %get-tuple-element.242) | copy-start | bytes 6148
Sparse Core Ops, SparseCore 0:
  200.8 56.4 reduce-scatter.1
  273.4 55.4 all-gather.3
where the time goes:
time: 653 us; the launch traced here: 645 us
  local copies, waits for them, and re-layouts  336 us (51%)
  blocking collectives  126 us (19%)
  waiting for transfers between devices  75 us (11%)
  matrix products  68.2 us (10%)
  between operations  14.5 us (2%)
  other arithmetic  14.2 us (2%)
  starting transfers between devices  10.2 us (2%)
    reshape x2, local copies, waits for them, and re-layouts, toeplitz_rows(): tiled[:row_count * (period - 1)]  86.4 us
    unnamed x28, local copies, waits for them, and re-layouts  83.3 us
    slice x2, local copies, waits for them, and re-layouts, toeplitz_rows(): tiled[:row_count * (period - 1)]  77.4 us
    psum x1, blocking collectives, broadcast(): return lax.psum(block, axis)  59.4 us
    reduce_scatter x1, waiting for transfers between devices, local(): lax.psum_scatter(partial_value.astype(jnp.bfloat16), 'chan', scatter_dime...  56.5 us
    all_gather x2, blocking collectives, entering_2(): lax.all_gather(part.astype(kind), axis)  53.7 us
    slice x2, local copies, waits for them, and re-layouts, toeplitz_rows(): return shaped[:, :col_count]  46.3 us
    another operation x2, local copies, waits for them, and re-layouts, toeplitz_rows(): tiled = jnp.tile(period_rows, (row_count, 1))  37.8 us
  transfers between devices with their start and end apart: 5, of which 2 were waited for; matrix products, arithmetic and copies ran while one was open for 53% of the time, Pallas kernels for 0%

commit v1 on v0

v1 whole, which is shorter than its diff:
```python
import functools

import jax
import jax.numpy as jnp
import ml_dtypes
import numpy as np
from jax import lax
from jax.experimental import pallas as pl
from jax.experimental.pallas import tpu as pltpu
from jax.sharding import PartitionSpec as P

MESH = pl.DeviceIdType.MESH
F32 = jnp.float32
BF16 = jnp.bfloat16

D = 4096
MODES = 16
CB = 32
EPSILON = 1e-06
BIG = 1e30

R = 256
W = 512
H = 16
N = 8

LATE = ((128, 48, (0, 1, 2)), (176, 48, (1, 2, 0)), (224, 32, (2, 0, 1)))
EARLY = ((0, 48, (0, 1, 2)), (48, 32, (1, 2, 0)), (80, 48, (2, 0, 1)))
PIECES = LATE + EARLY


def fourier(period, rows_in, out_from, rows_out):
    half = period // 2
    k = np.arange(half)[:, None]
    t = np.arange(rows_in)[None, :]
    angle = 2.0 * np.pi * ((k * t) % period) / period
    real, imag = np.cos(angle), -np.sin(angle)
    imag[0] = np.where(np.arange(rows_in) % 2 == 0, 1.0, -1.0)
    forward = np.concatenate([real, imag], axis=0)
    t = (out_from + np.arange(rows_out))[:, None]
    k = np.arange(half)[None, :]
    angle = 2.0 * np.pi * ((k * t) % period) / period
    real, imag = 2.0 * np.cos(angle), -2.0 * np.sin(angle)
    real[:, 0] = 1.0
    imag[:, 0] = np.where((out_from + np.arange(rows_out)) % 2 == 0, 1.0, -1.0)
    inverse = np.concatenate([real, imag], axis=1) / period
    return forward, inverse


def bits(slot):
    return (slot >> 2) & 1, (slot >> 1) & 1, slot & 1


def picked(**fixed):
    index = [slice(None)] * 3
    for name, value in fixed.items():
        index[2 - int(name[1])] = value
    return tuple(index)


def flipped(chan, slot):
    b2, b1, b0 = bits(slot)
    z, x = chan // 2, chan % 2
    if b0:
        x = 1 - x
    if b1:
        z = z + 1 - 2 * (z % 2)
    if b2:
        z = 3 - z
    return 2 * z + x


def kernel(
    n_seq,
    res_in, q_in, k_in, v_in, mix_in, liw_in,
    mr_short, mr_filter, gain, li_short, rate, residue, slots,
    f256, g256, f512, g512,
    li_out, res_out, dec_out,
    qkv, mu, qs, ht, gated, mw, part, rb1, rb2, rb3, res_v, hb, sqc, sqs, sqr,
    lw, lp, ql, ub, table, kern, lt, urev, conv, st, sb, sr, lo_v, ro_v,
    load_sem, halo_s, halo_r, rs_s, rs_r, ag_s, ag_r, sq_s, sq_r, st_s, st_r, out_sem,
):
    seq, chan = lax.axis_index("seq"), lax.axis_index("chan")
    first = seq == 0
    pending = []

    loads = []

    def load(src, dst):
        copy = pltpu.make_async_copy(src, dst, load_sem.at[len(loads)])
        copy.start()
        loads.append(copy)
        return copy

    in_loads = [load(ref, qkv.at[i, pl.ds(H, R), :]) for i, ref in enumerate((q_in, k_in, v_in))]
    mix_loads = [
        load(mix_in.at[:, pl.ds(pl.multiple_of(flipped(chan, s) * W, W), W)], mw.at[s]) for s in range(N)
    ]
    res_load = load(res_in, res_v)
    li_loads = [
        load(liw_in.at[:, pl.ds(pl.multiple_of(flipped(chan, s) * W, W), W), :], lw.at[:, pl.ds(s * W, W), :])
        for s in range(N)
    ]

    barrier = pltpu.get_barrier_semaphore()
    seq_peers = [lax.rem(seq + k, n_seq) for k in range(1, n_seq)]
    chan_peers = [lax.rem(chan + k, N) for k in range(1, N)]
    for peer in seq_peers:
        pl.semaphore_signal(barrier, inc=1, device_id=(peer, chan), device_id_type=MESH)
    for peer in chan_peers:
        pl.semaphore_signal(barrier, inc=1, device_id=(seq, peer), device_id_type=MESH)
    pl.semaphore_wait(barrier, n_seq - 1 + N - 1)

    def send(src, dst, send_sem, recv_sem, to):
        copy = pltpu.make_async_remote_copy(
            src_ref=src, dst_ref=dst, send_sem=send_sem, recv_sem=recv_sem,
            device_id=to, device_id_type=MESH,
        )
        copy.start()
        pending.append(copy)
        return copy

    after = (lax.rem(seq + 1, n_seq), chan)
    halos = [
        send(ref.at[pl.ds(R - H, H), :], qkv.at[i, pl.ds(0, H), :], halo_s.at[i], halo_r.at[i], after)
        for i, ref in enumerate((q_in, k_in, v_in))
    ]

    spectrum = jnp.dot(f256[:, :128], mr_filter[...], preferred_element_type=F32)
    row = lax.broadcasted_iota(jnp.int32, (128, W), 0)
    ht[0] = spectrum[:128]
    ht[1] = jnp.where(row == 0, 0.0, spectrum[128:])
    ht[2] = jnp.where(row == 0, spectrum[128:], spectrum[:128])

    def short(ext, taps, rows):
        once = pltpu.roll(ext, 1, 0)
        twice = pltpu.roll(ext, 2, 0)
        top = ext.shape[0] - rows
        return taps[0:1] * ext[top:] + taps[1:2] * once[top:] + taps[2:3] * twice[top:]

    for copy in in_loads:
        copy.wait()
    for copy in halos:
        copy.wait_recv()
    mr_taps = [mr_short[i].astype(F32) for i in range(3)]
    ext_row = lax.broadcasted_iota(jnp.int32, (H + R, 128), 0)
    outside = jnp.logical_and(first, ext_row < H)
    for c in range(W // 128):
        lanes = slice(c * 128, (c + 1) * 128)
        three = []
        for i in range(3):
            ext = jnp.where(outside, 0.0, qkv[i, :, lanes].astype(F32))
            three.append(short(ext, mr_taps[i][:, lanes], R))
        qs[:, lanes] = three[0]
        mu[128:, lanes] = (three[1] * three[2]).astype(BF16)
    rim = send(mu.at[pl.ds(R, 128), :], mu.at[pl.ds(0, 128), :], halo_s.at[3], halo_r.at[3], after)

    def mr_rows(r0):
        x = jnp.dot(f256[...], mu[r0 : r0 + 256, :], preferred_element_type=F32)
        xr, xi = x[:128], x[128:]
        y = jnp.concatenate(
            [
                (xr * ht[0] - xi * ht[1]).astype(BF16),
                (xr * ht[1] + xi * ht[2]).astype(BF16),
            ],
            axis=0,
        )
        out = jnp.dot(g256[...], y, preferred_element_type=F32)
        gated[r0 : r0 + 128, :] = (qs[r0 : r0 + 128, :] * out).astype(BF16)
        for s in range(N):
            part[bits(s) + (slice(r0, r0 + 128), slice(None))] = jnp.dot(
                gated[r0 : r0 + 128, :], mw[s], preferred_element_type=F32
            ).astype(BF16)

    def rs_view(ref, g, *fixed):
        r0, n, order = PIECES[g]
        index = picked(**{f"b{order[i]}": v for i, v in enumerate(fixed)})
        return index + (pl.ds(r0, n), slice(None))

    def rs_send(g, step):
        r0, n, order = PIECES[g]
        fixed = (0,) * step + (1,)
        src = part.at[rs_view(part, g, *fixed)]
        rows = pl.ds(r0, n)
        dst = (rb1.at[:, :, rows, :], rb2.at[:, rows, :], rb3.at[rows, :])[step]
        to = (seq, flipped(chan, 1 << order[step]))
        return send(src, dst, rs_s.at[g, step], rs_r.at[g, step], to)

    def rs_add(g, step):
        r0, n, order = PIECES[g]
        rows = slice(r0, r0 + n)
        fixed = (0,) * (step + 1)
        index = rs_view(part, g, *fixed)[:3] + (rows, slice(None))
        got = (rb1[:, :, rows, :], rb2[:, rows, :])[step]
        part[index] = (part[index].astype(F32) + got.astype(F32)).astype(BF16)

    def rs_end(g):
        r0, n, order = PIECES[g]
        rows = slice(r0, r0 + n)
        total = res_v[rows, :].astype(F32) + (
            part[0, 0, 0, rows, :].astype(F32) + rb3[rows, :].astype(F32)
        )
        ro_v[rows, :] = total.astype(BF16)
        sqc[rows, :] = jnp.broadcast_to(jnp.sum(total * total, axis=1, keepdims=True), (n, 128))
        scaled = jnp.clip(total * gain[...].astype(F32), -BIG, BIG)
        hb[0, 0, 0, rows, :] = scaled.astype(BF16)

    def ag_send(g, step):
        r0, n, order = PIECES[g]
        dims = order[::-1]
        later = {f"b{d}": 0 for d in dims[step + 1 :]}
        rows = (pl.ds(r0, n), slice(None))
        src = hb.at[picked(**later, **{f"b{dims[step]}": 0}) + rows]
        dst = hb.at[picked(**later, **{f"b{dims[step]}": 1}) + rows]
        to = (seq, flipped(chan, 1 << dims[step]))
        return send(src, dst, ag_s.at[g, step], ag_r.at[g, step], to)

    def sq_send(b, r0):
        sqs[b] = sqc[r0 : r0 + 128, :].T[:8]
        return [
            send(sqs.at[b], sqr.at[b, k], sq_s.at[b, k], sq_r.at[b, k], (seq, chan_peers[k]))
            for k in range(N - 1)
        ]

    def project(b, r0, squares):
        for copy in squares:
            copy.wait_recv()
        total = sqs[b]
        for k in range(N - 1):
            total = total + sqr[b, k]
        inverse = lax.rsqrt(total / D + EPSILON)
        inverse = jnp.broadcast_to(inverse[0:1], (128, 128)).T
        wide = jnp.concatenate([inverse] * (W // 128), axis=1)
        rows = slice(r0, r0 + 128)
        lhs = jnp.concatenate([hb[bits(s) + (rows, slice(None))] for s in range(N)], axis=1)

        def one(i, carry):
            out = jnp.dot(lhs, lw[i], preferred_element_type=F32) * wide
            lp[i, H + r0 : H + r0 + 128, :] = out.astype(BF16)
            return carry

        lax.fori_loop(0, 3, one, 0)

    late, early = range(3), range(3, 6)

    for copy in mix_loads:
        copy.wait()
    mr_rows(128)
    rs = {(g, 0): rs_send(g, 0) for g in late}
    rim.wait_recv()
    mu[:128, :] = jnp.where(first, jnp.zeros((128, W), BF16), mu[:128, :])
    mr_rows(0)
    rs.update({(g, 0): rs_send(g, 0) for g in early})

    kern[...] = jnp.zeros((R, W), F32)
    time = lax.broadcasted_iota(jnp.int32, (R, W), 0).astype(F32)

    def mode(m, carry):
        powers = jnp.exp(-rate[pl.ds(m, 1), :] * time)
        table[m] = powers
        kern[...] += residue[pl.ds(m, 1), :] * powers
        return carry

    lax.fori_loop(0, MODES // 2, mode, 0)

    for group in (late, early):
        for g in group:
            rs[g, 0].wait_recv()
            rs_add(g, 0)
            rs[g, 1] = rs_send(g, 1)

    lax.fori_loop(MODES // 2, MODES, mode, 0)
    spectrum = jnp.dot(f512[:512, :], kern[...].astype(BF16), preferred_element_type=F32)
    row = lax.broadcasted_iota(jnp.int32, (256, W), 0)
    lt[0] = spectrum[:256]
    lt[1] = jnp.where(row == 0, 0.0, spectrum[256:])
    lt[2] = jnp.where(row == 0, spectrum[256:], spectrum[:256])

    for group in (late, early):
        for g in group:
            rs[g, 1].wait_recv()
            rs_add(g, 1)
            rs[g, 2] = rs_send(g, 2)
    res_load.wait()
    ag = {}
    squares = []
    for b, group in enumerate((late, early)):
        for g in group:
            rs[g, 2].wait_recv()
            rs_end(g)
            ag[g, 0] = ag_send(g, 0)
        squares.append(sq_send(b, PIECES[group[0]][0]))
    res_store = pltpu.make_async_copy(ro_v, res_out, out_sem.at[0])
    res_store.start()
    for step in (1, 2):
        for group in (late, early):
            for g in group:
                ag[g, step - 1].wait_recv()
                ag[g, step] = ag_send(g, step)
    for copy in li_loads:
        copy.wait()
    for g in late:
        ag[g, 2].wait_recv()
    project(0, 128, squares[0])
    li_halo = send(lp.at[:, pl.ds(R, H), :], lp.at[:, pl.ds(0, H), :], halo_s.at[4], halo_r.at[4], after)
    for g in early:
        ag[g, 2].wait_recv()
    project(1, 0, squares[1])
    li_halo.wait_recv()

    li_taps = [li_short[i].astype(F32) for i in range(3)]
    for c in range(W // 128):
        lanes = slice(c * 128, (c + 1) * 128)
        three = []
        for i in range(3):
            ext = jnp.where(outside, 0.0, lp[i, :, lanes].astype(F32))
            three.append(short(ext, li_taps[i][:, lanes], R))
        ql[:, lanes] = three[0]
        ub[:, lanes] = (three[1] * three[2]).astype(BF16)
    urev[...] = jnp.dot(f512[512:, :], ub[...], preferred_element_type=F32)

    def ends(j, carry):
        for i in range(4):
            m = 4 * j + i
            st[pl.ds(m, 1), :] = jnp.sum(table[m] * urev[...], axis=0, keepdims=True)
        return carry

    lax.fori_loop(0, MODES // 4, ends, 0)
    sb[...] = st[...].astype(BF16)
    states = [
        send(sb, sr.at[k + 1], st_s.at[k], st_r.at[k], (seq_peers[k], chan)) for k in range(n_seq - 1)
    ]
    sr[0] = sb[...]

    x = jnp.dot(f512[:512, :], ub[...], preferred_element_type=F32)
    xr, xi = x[:256], x[256:]
    y = jnp.concatenate(
        [
            (xr * lt[0] - xi * lt[1]).astype(BF16),
            (xr * lt[1] + xi * lt[2]).astype(BF16),
        ],
        axis=0,
    )
    conv[...] = jnp.dot(g512[...], y, preferred_element_type=F32)

    for copy in states:
        copy.wait_recv()
    decay = jnp.exp(-rate[...] * float(R))
    zero = jnp.zeros((MODES, W), F32)
    incoming = zero
    for k in range(n_seq - 1, 0, -1):
        incoming = incoming * decay + jnp.where(seq >= k, sr[k].astype(F32), zero)
    st[...] = incoming * residue[...] * jnp.exp(-rate[...])

    def across(j, carry):
        rows = pl.ds(pl.multiple_of(j * 32, 32), 32)
        total = conv[rows, :]
        for m in range(MODES):
            total = total + st[m : m + 1, :] * table[m, rows, :]
        lo_v[rows, :] = (ql[rows, :] * total).astype(BF16)
        return carry

    lax.fori_loop(0, R // 32, across, 0)
    li_store = pltpu.make_async_copy(lo_v, li_out, out_sem.at[1])
    li_store.start()

    final = zero
    for j in range(n_seq):
        final = final * decay + sr[lax.rem(seq + n_seq - j, n_seq)].astype(F32)
    final = final * residue[...]
    high = final.astype(BF16)
    low = (final - high.astype(F32)).astype(BF16)
    mine = seq * N + chan
    block = jnp.int32(0)
    for b in range(slots.shape[0]):
        block = block + jnp.where(slots[b] == mine, jnp.int32(b), jnp.int32(0))
    source = lax.broadcasted_iota(jnp.int32, (W, W), 0) - block * CB
    target = lax.broadcasted_iota(jnp.int32, (W, W), 1) // MODES
    choose = jnp.where(source == target, 1.0, 0.0).astype(BF16)
    chosen = jnp.dot(high, choose, preferred_element_type=F32) + jnp.dot(
        low, choose, preferred_element_type=F32
    )
    m_row = lax.broadcasted_iota(jnp.int32, (MODES, W), 0)
    m_lane = lax.broadcasted_iota(jnp.int32, (MODES, W), 1) % MODES
    dec_out[...] = jnp.sum(jnp.where(m_row == m_lane, chosen, 0.0), axis=0, keepdims=True)

    for copy in pending:
        copy.wait_send()
    res_store.wait()
    li_store.wait()


def local(n_seq, residual_in, mr_query, mr_key, mr_value, mr_short, mr_filter, mix_weight, norm_gain,
          li_weight, li_short, li_rate, li_residue, decode_slot):
    f256, g256 = fourier(256, 256, 128, 128)
    f512, g512 = fourier(512, 256, 0, 256)
    f512 = np.concatenate([f512, np.eye(256)[::-1]], axis=0)
    tables = [jnp.asarray(a.astype(np.float32).astype(ml_dtypes.bfloat16)) for a in (f256, g256, f512, g512)]
    any_spec = pl.BlockSpec(memory_space=pl.ANY)
    vmem = pl.BlockSpec(memory_space=pltpu.VMEM)
    smem = pl.BlockSpec(memory_space=pltpu.SMEM)
    v = pltpu.VMEM
    dma = pltpu.SemaphoreType.DMA
    return pl.pallas_call(
        functools.partial(kernel, n_seq),
        out_shape=(
            jax.ShapeDtypeStruct((R, W), BF16),
            jax.ShapeDtypeStruct((R, W), BF16),
            jax.ShapeDtypeStruct((1, CB * MODES), F32),
        ),
        in_specs=[any_spec] * 6 + [vmem] * 6 + [smem] + [vmem] * 4,
        out_specs=(any_spec, any_spec, vmem),
        scratch_shapes=[
            v((3, H + R, W), BF16),
            v((128 + R, W), BF16),
            v((R, W), F32),
            v((3, 128, W), F32),
            v((R, W), BF16),
            v((N, W, W), BF16),
            v((2, 2, 2, R, W), BF16),
            v((2, 2, R, W), BF16),
            v((2, R, W), BF16),
            v((R, W), BF16),
            v((R, W), BF16),
            v((2, 2, 2, R, W), BF16),
            v((R, 128), F32),
            v((2, 8, 128), F32),
            v((2, N - 1, 8, 128), F32),
            v((3, N * W, W), BF16),
            v((3, H + R, W), BF16),
            v((R, W), F32),
            v((R, W), BF16),
            v((MODES, R, W), F32),
            v((R, W), F32),
            v((3, 256, W), F32),
            v((R, W), F32),
            v((R, W), F32),
            v((MODES, W), F32),
            v((MODES, W), BF16),
            v((n_seq, MODES, W), BF16),
            v((R, W), BF16),
            v((R, W), BF16),
            dma((20,)),
            dma((5,)), dma((5,)),
            dma((6, 3)), dma((6, 3)),
            dma((6, 3)), dma((6, 3)),
            dma((2, N - 1)), dma((2, N - 1)),
            dma((n_seq - 1,)), dma((n_seq - 1,)),
            dma((2,)),
        ],
        compiler_params=pltpu.CompilerParams(
            collective_id=0, has_side_effects=True, vmem_limit_bytes=60 * 1024 * 1024
        ),
        name="layers",
    )(
        residual_in, mr_query, mr_key, mr_value, mix_weight, li_weight,
        mr_short, mr_filter, norm_gain.reshape(1, W), li_short, li_rate.T, li_residue.T, decode_slot,
        *tables,
    )


def solution(mesh):
    in_specs = (
        P("seq", "chan"), P("seq", "chan"), P("seq", "chan"), P("seq", "chan"),
        P(None, None, "chan"), P(None, "chan"), P("chan", None), P("chan"),
        P(None, None, "chan"), P(None, None, "chan"), P("chan", None), P("chan", None), P("chan"),
    )
    out_specs = (P("seq", "chan"), P("seq", "chan"), P(("seq", "chan"), None))
    return jax.shard_map(
        functools.partial(local, mesh.shape["seq"]),
        mesh=mesh, in_specs=in_specs, out_specs=out_specs, check_vma=False,
    )
```

time: 653 us -> 65.7 us (0.10); the launches traced: 645 us -> 65.4 us
  local copies, waits for them, and re-layouts: 336 us -> 5.85 us
  blocking collectives: 126 us -> 0 us
  waiting for transfers between devices: 75 us -> 0 us
  matrix products: 68.2 us -> 0 us
  Pallas kernels: 0 us -> 58.9 us
  other arithmetic: 14.2 us -> 0 us
  between operations: 14.5 us -> 0.64 us
  starting transfers between devices: 10.2 us -> 0 us
    slice x11 -> x0, local copies, waits for them, and re-layouts: 124 us -> none  [the longest x2 77.4 us: toeplitz_rows(): tiled[:row_count * (period - 1)]]
    reshape x5 -> x1, local copies, waits for them, and re-layouts: 87 us -> 1.26 us  [local(): norm_gain.reshape(1, W)]
    unnamed x28 -> x3, local copies, waits for them, and re-layouts: 83.3 us -> 4.59 us
    psum x2 -> x0, blocking collectives: 72.5 us -> none  [the longest x1 59.4 us: broadcast(): return lax.psum(block, axis)]
    dot_general x7 -> x0, matrix products: 68.2 us -> none  [the longest x1 29.8 us: local(): jnp.einsum('tsc,bsc->btc', lower_band, input_blocks, precision=HIGHEST_PR...]
    pallas_call x0 -> x1, Pallas kernels: none -> 58.9 us  [local(): pl.pallas_call(functools.partial(kernel, n_seq), out_shape=(jax.ShapeDtyp...]
    reduce_scatter x1 -> x0, waiting for transfers between devices: 56.5 us -> none  [local(): lax.psum_scatter(partial_value.astype(jnp.bfloat16), 'chan', scatter_dime...]
    all_gather x2 -> x0, blocking collectives: 53.7 us -> none  [entering_2(): lax.all_gather(part.astype(kind), axis)]
  transfers between devices with their start and end apart: 5 -> 0, of which waited for: 2 -> 0; matrix products, arithmetic and copies ran while one was open for 53% -> 0% of each run, Pallas kernels for 0% -> 0%
where the time goes in v1:
time: 65.7 us; the launch traced here: 65.4 us
  Pallas kernels  58.9 us (90%)
  local copies, waits for them, and re-layouts  5.85 us (9%)
    pallas_call x1, Pallas kernels, local(): pl.pallas_call(functools.partial(kernel, n_seq), out_shape=(jax.ShapeDtyp...  58.9 us
    unnamed x3, local copies, waits for them, and re-layouts  4.59 us

profile of v1, /device:TPU:1, one launch (start us, length us, event | category | flops | bytes accessed | tf_op | source)
XLA Modules:
  0.0 65.4 jit_solution(13756336578323220573)
XLA Ops:
  0.6 1.3 %reshape.9.gain = bf16[1,512]{1,0:T(2,128)(2,1)} reshape(bf16[512]{0:T(512)(128)(2,1)} %param.24) | data formatting | bytes 2048 | tf_op jit(solution)/shard_map/reshape | solution.py:457
  1.9 58.9 %layers.1 = (bf16[256,512]{1,0:T(8,128)(2,1)}, bf16[256,512]{1,0:T(8,128)(2,1)}, f32[1,512]{1,0:T(1,128)}) custom-call(bf16[256,512]{1,0:T(8,128)(2,1)} %res_in.1, bf16[256,512]{1,0:T(8,128)(2,1)} %q_in.1, bf16[256,512]{1,0:T(8,128)(2,1)} %k_in.1, bf16[256,512]{1,0:T(8,128)(2,1)} %v_in.1, bf16[512,4096]{1,0:T(8,128)(2,1)} %mix_in.1, ...), custom_call_target="tpu_custom_call" | custom-call | tf_op jit(solution)/shard_map/layers/pallas_call | solution.py:404
  60.8 1.7 %copy.23 = bf16[256,512]{1,0:T(8,128)(2,1)} copy(bf16[256,512]{1,0:T(8,128)(2,1)} %get-tuple-element.6) | data formatting | bytes 524288
  62.5 1.7 %copy.24 = bf16[256,512]{1,0:T(8,128)(2,1)} copy(bf16[256,512]{1,0:T(8,128)(2,1)} %get-tuple-element.7) | data formatting | bytes 524288
  64.2 1.3 %copy.25 = f32[1,512]{1,0:T(1,128)} copy(f32[1,512]{1,0:T(1,128)} %get-tuple-element.8) | data formatting | bytes 4096

commit v2 on v1

v2 whole, which is shorter than its diff:
```python
import functools

import jax
import jax.numpy as jnp
import ml_dtypes
import numpy as np
from jax import lax
from jax.experimental import pallas as pl
from jax.experimental.pallas import tpu as pltpu
from jax.sharding import PartitionSpec as P

MESH = pl.DeviceIdType.MESH
F32 = jnp.float32
BF16 = jnp.bfloat16

D = 4096
MODES = 16
CB = 32
EPSILON = 1e-06
BIG = 1e30

R = 256
W = 512
H = 16
N = 8

SPLIT = 144
BATCHES = (
    ((144, 16, (0, 1, 2)), (160, 16, (1, 2, 0)), (176, 16, (2, 0, 1))),
    ((192, 32, (0, 1, 2)), (224, 16, (1, 2, 0)), (240, 16, (2, 0, 1))),
    ((0, 16, (0, 1, 2)), (16, 32, (1, 2, 0)), (48, 32, (2, 0, 1))),
    ((80, 32, (0, 1, 2)), (112, 16, (1, 2, 0)), (128, 16, (2, 0, 1))),
)
PIECES = sum(BATCHES, ())


def fourier(period, rows_in, out_from, rows_out):
    half = period // 2
    k = np.arange(half)[:, None]
    t = np.arange(rows_in)[None, :]
    angle = 2.0 * np.pi * ((k * t) % period) / period
    real, imag = np.cos(angle), -np.sin(angle)
    imag[0] = np.where(np.arange(rows_in) % 2 == 0, 1.0, -1.0)
    forward = np.concatenate([real, imag], axis=0)
    t = (out_from + np.arange(rows_out))[:, None]
    k = np.arange(half)[None, :]
    angle = 2.0 * np.pi * ((k * t) % period) / period
    real, imag = 2.0 * np.cos(angle), -2.0 * np.sin(angle)
    real[:, 0] = 1.0
    imag[:, 0] = np.where((out_from + np.arange(rows_out)) % 2 == 0, 1.0, -1.0)
    inverse = np.concatenate([real, imag], axis=1) / period
    return forward, inverse


def bits(slot):
    return (slot >> 2) & 1, (slot >> 1) & 1, slot & 1


def picked(**fixed):
    index = [slice(None)] * 3
    for name, value in fixed.items():
        index[2 - int(name[1])] = value
    return tuple(index)


def flipped(chan, slot):
    b2, b1, b0 = bits(slot)
    z, x = chan // 2, chan % 2
    if b0:
        x = 1 - x
    if b1:
        z = z + 1 - 2 * (z % 2)
    if b2:
        z = 3 - z
    return 2 * z + x


def kernel(
    n_seq,
    res_in, q_in, k_in, v_in, mix_in, liw_in, filter_in, f256_in, g256_in, f512_in, g512_in, rate_in, residue_in,
    mr_short, li_short, gain, slots,
    li_out, res_out, dec_out,
    qkv, mu, qs, ht, gated, mw, part, rb1, rb2, rb3, res_v, hb, gains, inv_gains,
    lw, lp, ql, ub, table, back, kern, lt, conv, st, sb, sr, lo_v, ro_v,
    mr_filter, f256, g256, f512, g512, rate, residue,
    load_sem, halo_s, halo_r, rs_s, rs_r, ag_s, ag_r, gain_s, gain_r, st_s, st_r, out_sem,
):
    seq, chan = lax.axis_index("seq"), lax.axis_index("chan")
    first = seq == 0
    pending = []

    loads = []

    def load(src, dst):
        copy = pltpu.make_async_copy(src, dst, load_sem.at[len(loads)])
        copy.start()
        loads.append(copy)
        return copy

    first_loads = [load(filter_in, mr_filter), load(f256_in, f256)]
    in_loads = [load(ref, qkv.at[i, pl.ds(H, R), :]) for i, ref in enumerate((q_in, k_in, v_in))]
    g_load = load(g256_in, g256)
    mix_loads = [
        load(mix_in.at[:, pl.ds(pl.multiple_of(flipped(chan, s) * W, W), W)], mw.at[s]) for s in range(N)
    ]

    barrier = pltpu.get_barrier_semaphore()
    after = (lax.rem(seq + 1, n_seq), chan)
    chan_peers = [(seq, flipped(chan, s)) for s in range(1, N)]
    seq_peers = [(lax.rem(seq + k, n_seq), chan) for k in range(1, n_seq)]
    for peer in chan_peers + seq_peers:
        pl.semaphore_signal(barrier, inc=1, device_id=peer, device_id_type=MESH)

    def send(src, dst, send_sem, recv_sem, to):
        copy = pltpu.make_async_remote_copy(
            src_ref=src, dst_ref=dst, send_sem=send_sem, recv_sem=recv_sem,
            device_id=to, device_id_type=MESH,
        )
        copy.start()
        pending.append(copy)
        return copy

    for copy in first_loads:
        copy.wait()
    spectrum = jnp.dot(f256[:, :128], mr_filter[...], preferred_element_type=F32)
    row = lax.broadcasted_iota(jnp.int32, (128, W), 0)
    ht[0] = spectrum[:128]
    ht[1] = jnp.where(row == 0, 0.0, spectrum[128:])
    ht[2] = jnp.where(row == 0, spectrum[128:], spectrum[:128])

    mode_loads = [load(rate_in, rate), load(residue_in, residue)]
    own_gain = gain[...].astype(F32).reshape(1, W)
    gains[0] = own_gain

    def short(ext, taps, rows):
        once = pltpu.roll(ext, 1, 0)
        twice = pltpu.roll(ext, 2, 0)
        top = ext.shape[0] - rows
        return taps[0:1] * ext[top:] + taps[1:2] * once[top:] + taps[2:3] * twice[top:]

    for copy in in_loads:
        copy.wait()
    mr_taps = [mr_short[i].astype(F32) for i in range(3)]
    for c in range(W // 128):
        lanes = slice(c * 128, (c + 1) * 128)
        three = [short(qkv[i, H:, lanes].astype(F32), mr_taps[i][:, lanes], R) for i in range(3)]
        qs[:, lanes] = three[0]
        mu[128:, lanes] = (three[1] * three[2]).astype(BF16)

    def filtered(r0):
        x = jnp.dot(f256[...], mu[r0 : r0 + 256, :], preferred_element_type=F32)
        xr, xi = x[:128], x[128:]
        y = jnp.concatenate(
            [
                (xr * ht[0] - xi * ht[1]).astype(BF16),
                (xr * ht[1] + xi * ht[2]).astype(BF16),
            ],
            axis=0,
        )
        return jnp.dot(g256[...], y, preferred_element_type=F32)

    def mixed(r0, r1):
        for s in range(N):
            part[bits(s) + (slice(r0, r1), slice(None))] = jnp.dot(
                gated[r0:r1, :], mw[s], preferred_element_type=F32
            ).astype(BF16)

    def fixed_bits(g, count, last=0):
        order = PIECES[g][2]
        bit = {f"b{d}": 0 for d in order[:count]}
        if last:
            bit[f"b{order[count]}"] = 1
        return picked(**bit)

    def step_send(g, step):
        r0, n, order = PIECES[g]
        rows = (pl.ds(r0, n), slice(None))
        dim = order[(0, 1, 2, 1, 0)[step]]
        to = (seq, flipped(chan, 1 << dim))
        if step < 2:
            src = part.at[fixed_bits(g, step, 1) + rows]
            dst = rb1.at[(slice(None),) * 2 + rows] if step == 0 else rb2.at[(slice(None),) + rows]
            return send(src, dst, rs_s.at[g, step], rs_r.at[g, step], to)
        if step == 2:
            src = part.at[fixed_bits(g, 2) + rows]
            return send(src, rb3.at[(slice(None),) + rows], rs_s.at[g, 2], rs_r.at[g, 2], to)
        kept = 1 if step == 3 else 0
        src = hb.at[fixed_bits(g, kept + 1) + rows]
        dst = hb.at[fixed_bits(g, kept, 1) + rows]
        return send(src, dst, ag_s.at[g, step - 3], ag_r.at[g, step - 3], to)

    def step_work(g, step):
        r0, n, order = PIECES[g]
        rows = (slice(r0, r0 + n), slice(None))
        if step == 1:
            index = fixed_bits(g, 1) + rows
            part[index] = (part[index].astype(F32) + rb1[(slice(None),) * 2 + rows].astype(F32)).astype(BF16)
        if step in (2, 3):
            near = (0, 0, 0) + rows
            far = bits(1 << order[2]) + rows
        if step == 2:
            part[near] = (
                part[near].astype(F32) + rb2[(0,) + rows].astype(F32) + res_v[rows].astype(F32)
            ).astype(BF16)
            part[far] = (part[far].astype(F32) + rb2[(1,) + rows].astype(F32)).astype(BF16)
        if step == 3:
            total = part[near].astype(F32) + rb3[(1,) + rows].astype(F32)
            ro_v[rows] = total.astype(BF16)
            hb[near] = jnp.clip(total * gains[0], -BIG, BIG).astype(BF16)
            total = part[far].astype(F32) + rb3[(0,) + rows].astype(F32)
            hb[far] = jnp.clip(total * gains[1 << order[2]], -BIG, BIG).astype(BF16)

    flying = {}

    def advance(b, step):
        for g in range(3 * b, 3 * b + 3):
            if step > 0:
                flying[g, step - 1].wait_recv()
                step_work(g, step)
            flying[g, step] = step_send(g, step)

    def row_scale(r0, r1):
        squares = jnp.zeros((r1 - r0, 128), F32)
        for s in range(N):
            sums = hb[bits(s) + (slice(r0, r1), slice(None))].astype(F32) * inv_gains[s]
            sums = sums * sums
            for c in range(W // 128):
                squares = squares + sums[:, c * 128 : (c + 1) * 128]
        return lax.rsqrt(jnp.sum(squares, axis=1, keepdims=True) / D + EPSILON)

    def project(r0, r1, inverse, which):
        lhs = jnp.concatenate([hb[bits(s) + (slice(r0, r1), slice(None))] for s in range(N)], axis=1)
        for i in which:
            out = jnp.dot(lhs, lw[i], preferred_element_type=F32) * inverse
            lp[i, H + r0 : H + r1, :] = out.astype(BF16)

    kern[...] = jnp.zeros((R, W), F32)
    time = lax.broadcasted_iota(jnp.int32, (R, W), 0).astype(F32)

    def modes(first_mode, count):
        def mode(m, carry):
            powers = jnp.exp(-rate[pl.ds(m, 1), :] * time)
            table[m] = powers
            kern[...] += residue[pl.ds(m, 1), :] * powers
            back[m] = jnp.exp(-rate[pl.ds(m, 1), :] * (R - 1.0 - time))
            return carry

        lax.fori_loop(first_mode, first_mode + count, mode, 0)

    def kernel_spectrum():
        spectrum = jnp.dot(f512[...], kern[...].astype(BF16), preferred_element_type=F32)
        row = lax.broadcasted_iota(jnp.int32, (256, W), 0)
        lt[0] = spectrum[:256]
        lt[1] = jnp.where(row == 0, 0.0, spectrum[256:])
        lt[2] = jnp.where(row == 0, spectrum[256:], spectrum[:256])

    li_taps = []

    def li_short_rows(i, r0, r1, lanes):
        ext = lp[i, r0 : H + r1, lanes].astype(F32)
        if r0 == 0:
            ext_row = lax.broadcasted_iota(jnp.int32, ext.shape, 0)
            ext = jnp.where(jnp.logical_and(first, ext_row < H), 0.0, ext)
        return short(ext, li_taps[i][:, lanes], r1 - r0)

    def li_queries(r0, r1):
        for c in range(W // 128):
            lanes = slice(c * 128, (c + 1) * 128)
            ql[r0:r1, lanes] = li_short_rows(0, r0, r1, lanes)

    def li_inputs(r0, r1):
        for c in range(W // 128):
            lanes = slice(c * 128, (c + 1) * 128)
            product = li_short_rows(1, r0, r1, lanes) * li_short_rows(2, r0, r1, lanes)
            ub[r0:r1, lanes] = product.astype(BF16)
        values = ub[r0:r1, :].astype(F32)

        def ends(j, carry):
            for i in range(4):
                m = 4 * j + i
                st[pl.ds(m, 1), :] += jnp.sum(back[m, r0:r1, :] * values, axis=0, keepdims=True)
            return carry

        lax.fori_loop(0, MODES // 4, ends, 0)

    g_load.wait()
    out = filtered(128)
    gated[SPLIT:, :] = (qs[SPLIT:, :] * out[SPLIT - 128 :]).astype(BF16)
    pl.semaphore_wait(barrier, N - 1 + n_seq - 1)
    halos = [
        send(qkv.at[i, pl.ds(R, H), :], qkv.at[i, pl.ds(0, H), :], halo_s.at[i], halo_r.at[i], after)
        for i in range(3)
    ]
    rim = send(mu.at[pl.ds(R, 128), :], mu.at[pl.ds(0, 128), :], halo_s.at[3], halo_r.at[3], after)
    for copy in mix_loads:
        copy.wait()
    mixed(SPLIT, 192)
    advance(0, 0)
    mixed(192, R)
    advance(1, 0)

    gain_sends = [
        send(gains.at[0], gains.at[s], gain_s.at[s - 1], gain_r.at[s - 1], chan_peers[s - 1])
        for s in range(1, N)
    ]
    res_load = load(res_in, res_v)
    more_loads = [load(f512_in, f512), load(g512_in, g512)]
    li_loads = [
        load(liw_in.at[:, pl.ds(pl.multiple_of(flipped(chan, s) * W, W), W), :], lw.at[:, pl.ds(s * W, W), :])
        for s in range(N)
    ]
    for copy in mode_loads:
        copy.wait()
    modes(0, 4)

    advance(0, 1)

    for copy in halos:
        copy.wait_recv()
    fixed = []
    ext_row = lax.broadcasted_iota(jnp.int32, (2 * H, W), 0)
    outside = jnp.logical_and(first, ext_row < H)
    for i in range(3):
        ext = jnp.where(outside, 0.0, qkv[i, : 2 * H, :].astype(F32))
        fixed.append(short(ext, mr_taps[i], H))
    qs[:H, :] = fixed[0]
    right = (fixed[1] * fixed[2]).astype(BF16)
    missed = (right.astype(F32) - mu[128 : 128 + H, :].astype(F32))[1:2] * mr_filter[127:128, :].astype(F32)
    mu[128 : 128 + H, :] = right
    ahead = out[: SPLIT - 128]
    ahead = ahead + jnp.where(lax.broadcasted_iota(jnp.int32, ahead.shape, 0) == 0, missed, 0.0)
    gated[128:SPLIT, :] = (qs[128:SPLIT, :] * ahead).astype(BF16)
    rim.wait_recv()
    mu[:128, :] = jnp.where(first, jnp.zeros((128, W), BF16), mu[:128, :])
    gated[:128, :] = (qs[:128, :] * filtered(0)).astype(BF16)
    mixed(0, 80)
    advance(2, 0)
    mixed(80, SPLIT)
    advance(3, 0)

    advance(1, 1)
    modes(4, 4)
    res_load.wait()
    for copy in gain_sends:
        copy.wait_recv()
    for s in range(N):
        inv_gains[s] = 1.0 / gains[s]
    advance(0, 2)
    modes(8, 4)
    advance(2, 1)
    advance(3, 1)
    advance(1, 2)
    advance(0, 3)
    modes(12, 4)
    advance(2, 2)
    advance(3, 2)
    advance(1, 3)
    advance(0, 4)
    for copy in more_loads:
        copy.wait()
    kernel_spectrum()
    advance(2, 3)
    advance(3, 3)
    advance(1, 4)
    res_store = pltpu.make_async_copy(ro_v, res_out, out_sem.at[0])
    res_store.start()
    for copy in li_loads:
        copy.wait()
    li_taps.extend(li_short[i].astype(F32) for i in range(3))
    st[...] = jnp.zeros((MODES, W), F32)
    advance(2, 4)
    advance(3, 4)

    def arrived(*batches):
        for b in batches:
            for g in range(3 * b, 3 * b + 3):
                flying[g, 4].wait_recv()

    arrived(0, 1)
    project(SPLIT, R, row_scale(SPLIT, R), (0, 1, 2))
    li_halo = send(lp.at[:, pl.ds(R, H), :], lp.at[:, pl.ds(0, H), :], halo_s.at[4], halo_r.at[4], after)
    li_inputs(160, R)
    li_queries(160, R)
    arrived(2, 3)
    inverse = row_scale(0, SPLIT)
    project(0, SPLIT, inverse, (1, 2))
    li_halo.wait_recv()
    li_inputs(0, 160)
    sb[...] = st[...].astype(BF16)
    states = [send(sb, sr.at[k + 1], st_s.at[k], st_r.at[k], seq_peers[k]) for k in range(n_seq - 1)]
    project(0, SPLIT, inverse, (0,))
    li_queries(0, 160)

    x = jnp.dot(f512[...], ub[...], preferred_element_type=F32)
    xr, xi = x[:256], x[256:]
    y = jnp.concatenate(
        [
            (xr * lt[0] - xi * lt[1]).astype(BF16),
            (xr * lt[1] + xi * lt[2]).astype(BF16),
        ],
        axis=0,
    )
    conv[...] = jnp.dot(g512[...], y, preferred_element_type=F32)

    sr[0] = sb[...]
    decay = jnp.exp(-rate[...] * float(R))
    leaving = residue[...] * jnp.exp(-rate[...])
    for copy in states:
        copy.wait_recv()
    incoming = jnp.zeros((MODES, W), F32)
    for k in range(n_seq - 1, 0, -1):
        incoming = incoming * decay + jnp.where(seq >= k, sr[k].astype(F32), 0.0)
    st[...] = incoming * leaving

    def across(j, carry):
        rows = pl.ds(pl.multiple_of(j * 32, 32), 32)
        total = conv[rows, :]
        for m in range(MODES):
            total = total + st[m : m + 1, :] * table[m, rows, :]
        lo_v[rows, :] = (ql[rows, :] * total).astype(BF16)
        return carry

    stores = [res_store]
    for i in range(2):
        lax.fori_loop(i * R // 64, (i + 1) * R // 64, across, 0)
        rows = pl.ds(i * (R // 2), R // 2)
        stores.append(pltpu.make_async_copy(lo_v.at[rows, :], li_out.at[rows, :], out_sem.at[1 + i]))
        stores[-1].start()

    final = jnp.zeros((MODES, W), F32)
    for j in range(n_seq):
        final = final * decay + sr[lax.rem(seq + n_seq - j, n_seq)].astype(F32)
    final = final * residue[...]
    high = final.astype(BF16)
    low = (final - high.astype(F32)).astype(BF16)
    mine = seq * N + chan
    block = jnp.int32(0)
    for b in range(slots.shape[0]):
        block = block + jnp.where(slots[b] == mine, jnp.int32(b), jnp.int32(0))
    source = lax.broadcasted_iota(jnp.int32, (W, W), 0) - block * CB
    target = lax.broadcasted_iota(jnp.int32, (W, W), 1) // MODES
    choose = jnp.where(source == target, 1.0, 0.0).astype(BF16)
    chosen = jnp.dot(high, choose, preferred_element_type=F32) + jnp.dot(
        low, choose, preferred_element_type=F32
    )
    m_row = lax.broadcasted_iota(jnp.int32, (MODES, W), 0)
    m_lane = lax.broadcasted_iota(jnp.int32, (MODES, W), 1) % MODES
    dec_out[...] = jnp.sum(jnp.where(m_row == m_lane, chosen, 0.0), axis=0, keepdims=True)

    for copy in pending:
        copy.wait_send()
    for copy in stores:
        copy.wait()


def hand_over(li_in, res_in, dec_in, li_out, res_out, dec_out, li_v, res_v, dec_v, sem):
    trips = ((li_in, li_v, li_out), (res_in, res_v, res_out), (dec_in, dec_v, dec_out))
    there = [pltpu.make_async_copy(src, held, sem.at[0, i]) for i, (src, held, _) in enumerate(trips)]
    again = [pltpu.make_async_copy(held, dst, sem.at[1, i]) for i, (_, held, dst) in enumerate(trips)]
    for copy in there:
        copy.start()
    for copy, later in zip(there, again):
        copy.wait()
        later.start()
    for copy in again:
        copy.wait()


def local(n_seq, residual_in, mr_query, mr_key, mr_value, mr_short, mr_filter, mix_weight, norm_gain,
          li_weight, li_short, li_rate, li_residue, decode_slot):
    f256, g256 = fourier(256, 256, 128, 128)
    f512, g512 = fourier(512, 256, 0, 256)
    tables = [jnp.asarray(a.astype(np.float32).astype(ml_dtypes.bfloat16)) for a in (f256, g256, f512, g512)]
    hbm = pl.BlockSpec(memory_space=pltpu.HBM)
    vmem = pl.BlockSpec(memory_space=pltpu.VMEM)
    smem = pl.BlockSpec(memory_space=pltpu.SMEM)
    v = pltpu.VMEM
    dma = pltpu.SemaphoreType.DMA
    shapes = (
        jax.ShapeDtypeStruct((R, W), BF16),
        jax.ShapeDtypeStruct((R, W), BF16),
        jax.ShapeDtypeStruct((1, CB * MODES), F32),
    )
    done = pl.pallas_call(
        functools.partial(kernel, n_seq),
        out_shape=shapes,
        in_specs=[hbm] * 13 + [vmem] * 3 + [smem],
        out_specs=(hbm, hbm, vmem),
        scratch_shapes=[
            v((3, H + R, W), BF16),
            v((128 + R, W), BF16),
            v((R, W), F32),
            v((3, 128, W), F32),
            v((R, W), BF16),
            v((N, W, W), BF16),
            v((2, 2, 2, R, W), BF16),
            v((2, 2, R, W), BF16),
            v((2, R, W), BF16),
            v((2, R, W), BF16),
            v((R, W), BF16),
            v((2, 2, 2, R, W), BF16),
            v((N, 1, W), F32),
            v((N, 1, W), F32),
            v((3, N * W, W), BF16),
            v((3, H + R, W), BF16),
            v((R, W), F32),
            v((R, W), BF16),
            v((MODES, R, W), F32),
            v((MODES, R, W), F32),
            v((R, W), F32),
            v((3, 256, W), F32),
            v((R, W), F32),
            v((MODES, W), F32),
            v((MODES, W), BF16),
            v((n_seq, MODES, W), BF16),
            v((R, W), BF16),
            v((R, W), BF16),
            v((128, W), BF16),
            v((256, 256), BF16),
            v((128, 256), BF16),
            v((512, 256), BF16),
            v((256, 512), BF16),
            v((MODES, W), F32),
            v((MODES, W), F32),
            dma((30,)),
            dma((5,)), dma((5,)),
            dma((len(PIECES), 3)), dma((len(PIECES), 3)),
            dma((len(PIECES), 2)), dma((len(PIECES), 2)),
            dma((N - 1,)), dma((N - 1,)),
            dma((n_seq - 1,)), dma((n_seq - 1,)),
            dma((3,)),
        ],
        compiler_params=pltpu.CompilerParams(
            collective_id=0, has_side_effects=True, vmem_limit_bytes=60 * 1024 * 1024
        ),
        name="layers",
    )(
        residual_in, mr_query, mr_key, mr_value, mix_weight, li_weight, mr_filter, *tables, li_rate.T, li_residue.T,
        mr_short, li_short, norm_gain, decode_slot,
    )
    return pl.pallas_call(
        hand_over,
        out_shape=shapes,
        in_specs=[hbm] * 3,
        out_specs=(hbm,) * 3,
        scratch_shapes=[v((R, W), BF16), v((R, W), BF16), v((1, CB * MODES), F32), dma((2, 3))],
        compiler_params=pltpu.CompilerParams(vmem_limit_bytes=60 * 1024 * 1024),
        name="hand_over",
    )(*done)


def solution(mesh):
    in_specs = (
        P("seq", "chan"), P("seq", "chan"), P("seq", "chan"), P("seq", "chan"),
        P(None, None, "chan"), P(None, "chan"), P("chan", None), P("chan"),
        P(None, None, "chan"), P(None, None, "chan"), P("chan", None), P("chan", None), P("chan"),
    )
    out_specs = (P("seq", "chan"), P("seq", "chan"), P(("seq", "chan"), None))
    return jax.shard_map(
        functools.partial(local, mesh.shape["seq"]),
        mesh=mesh, in_specs=in_specs, out_specs=out_specs, check_vma=False,
    )
```

time: 65.7 us -> 54.9 us (0.84)
  local copies, waits for them, and re-layouts: 5.85 us -> 0 us
  Pallas kernels: 58.9 us -> 54.1 us
    pallas_call x1 -> x2, Pallas kernels: 58.9 us -> 54.1 us  [the longest x1 52.3 us: local(): pl.pallas_call(functools.partial(kernel, n_seq), out_shape=shapes, in_spe...]
    unnamed x3 -> x0, local copies, waits for them, and re-layouts: 4.59 us -> none
    reshape x1 -> x0, local copies, waits for them, and re-layouts: 1.26 us -> none  [local(): norm_gain.reshape(1, W)]
where the time goes in v2:
time: 54.9 us; the launch traced here: 54.7 us
  Pallas kernels  54.1 us (99%)
  between operations  0.64 us (1%)
    pallas_call x1, Pallas kernels, local(): pl.pallas_call(functools.partial(kernel, n_seq), out_shape=shapes, in_spe...  52.3 us
    pallas_call x1, Pallas kernels, local(): pl.pallas_call(hand_over, out_shape=shapes, in_specs=[hbm] * 3, out_specs...  1.79 us

profile of v2, /device:TPU:1, one launch (start us, length us, event | category | flops | bytes accessed | tf_op | source)
XLA Modules:
  0.0 54.7 jit_solution(18287227407817729969)
XLA Ops:
  0.6 52.3 %layers.1 = (bf16[256,512]{1,0:T(8,128)(2,1)}, bf16[256,512]{1,0:T(8,128)(2,1)}, f32[1,512]{1,0:T(1,128)}) custom-call(bf16[256,512]{1,0:T(8,128)(2,1)} %res_in.1, bf16[256,512]{1,0:T(8,128)(2,1)} %q_in.1, bf16[256,512]{1,0:T(8,128)(2,1)} %k_in.1, bf16[256,512]{1,0:T(8,128)(2,1)} %v_in.1, bf16[512,4096]{1,0:T(8,128)(2,1)} %mix_in.1, ...), custom_call_target="tpu_custom_call" | custom-call | tf_op jit(solution)/shard_map/layers/pallas_call | solution.py:484
  52.9 1.8 %hand_over.1 = (bf16[256,512]{1,0:T(8,128)(2,1)}, bf16[256,512]{1,0:T(8,128)(2,1)}, f32[1,512]{1,0:T(1,128)}) custom-call(bf16[256,512]{1,0:T(8,128)(2,1)} %get-tuple-element.6.li_in, bf16[256,512]{1,0:T(8,128)(2,1)} %get-tuple-element.7.res_in, f32[1,512]{1,0:T(1,128)} %get-tuple-element.8.dec_in), custom_call_target="tpu_custom_call" | custom-call | tf_op jit(solution)/shard_map/hand_over/pallas_call | solution.py:541

commit v3 on v2

--- a/solution.py
+++ b/solution.py
@@ -78,31 +78,16 @@
 def kernel(
     n_seq,
     res_in, q_in, k_in, v_in, mix_in, liw_in, filter_in, f256_in, g256_in, f512_in, g512_in, rate_in, residue_in,
-    mr_short, li_short, gain, slots,
+    mr_short_in, li_short_in, gain_in, slots_in,
     li_out, res_out, dec_out,
     qkv, mu, qs, ht, gated, mw, part, rb1, rb2, rb3, res_v, hb, gains, inv_gains,
     lw, lp, ql, ub, table, back, kern, lt, conv, st, sb, sr, lo_v, ro_v,
-    mr_filter, f256, g256, f512, g512, rate, residue,
+    mr_filter, f256, g256, f512, g512, rate, residue, mr_short, li_short, gain, slots,
     load_sem, halo_s, halo_r, rs_s, rs_r, ag_s, ag_r, gain_s, gain_r, st_s, st_r, out_sem,
 ):
     seq, chan = lax.axis_index("seq"), lax.axis_index("chan")
     first = seq == 0
     pending = []
-
-    loads = []
-
-    def load(src, dst):
-        copy = pltpu.make_async_copy(src, dst, load_sem.at[len(loads)])
-        copy.start()
-        loads.append(copy)
-        return copy
-
-    first_loads = [load(filter_in, mr_filter), load(f256_in, f256)]
-    in_loads = [load(ref, qkv.at[i, pl.ds(H, R), :]) for i, ref in enumerate((q_in, k_in, v_in))]
-    g_load = load(g256_in, g256)
-    mix_loads = [
-        load(mix_in.at[:, pl.ds(pl.multiple_of(flipped(chan, s) * W, W), W)], mw.at[s]) for s in range(N)
-    ]
 
     barrier = pltpu.get_barrier_semaphore()
     after = (lax.rem(seq + 1, n_seq), chan)
@@ -111,14 +96,52 @@
     for peer in chan_peers + seq_peers:
         pl.semaphore_signal(barrier, inc=1, device_id=peer, device_id_type=MESH)
 
-    def send(src, dst, send_sem, recv_sem, to):
-        copy = pltpu.make_async_remote_copy(
+    loads = []
+
+    def load(src, dst):
+        copy = pltpu.make_async_copy(src, dst, load_sem.at[len(loads)])
+        copy.start()
+        loads.append(copy)
+        return copy
+
+    first_loads = [load(filter_in, mr_filter), load(f256_in, f256)]
+    in_loads = [load(mr_short_in, mr_short)] + [
+        load(ref, qkv.at[i, pl.ds(H, R), :]) for i, ref in enumerate((q_in, k_in, v_in))
+    ]
+    g_load = load(g256_in, g256)
+    mix_loads = [
+        load(mix_in.at[:, pl.ds(pl.multiple_of(flipped(chan, s) * W, W), W)], mw.at[s]) for s in range(N)
+    ]
+
+    def remote(src, dst, send_sem, recv_sem, to):
+        return pltpu.make_async_remote_copy(
             src_ref=src, dst_ref=dst, send_sem=send_sem, recv_sem=recv_sem,
             device_id=to, device_id_type=MESH,
         )
+
+    def send(*what):
+        copy = remote(*what)
         copy.start()
         pending.append(copy)
         return copy
+
+    def hand_on(*copies):
+        @pl.when(seq < n_seq - 1)
+        def _():
+            for copy in copies:
+                copy.start()
+
+    def handed(*copies):
+        @pl.when(seq > 0)
+        def _():
+            for copy in copies:
+                copy.wait_recv()
+
+    def handed_on(*copies):
+        @pl.when(seq < n_seq - 1)
+        def _():
+            for copy in copies:
+                copy.wait_send()
 
     for copy in first_loads:
         copy.wait()
@@ -128,9 +151,8 @@
     ht[1] = jnp.where(row == 0, 0.0, spectrum[128:])
     ht[2] = jnp.where(row == 0, spectrum[128:], spectrum[:128])
 
+    gain_load = load(gain_in, gain)
     mode_loads = [load(rate_in, rate), load(residue_in, residue)]
-    own_gain = gain[...].astype(F32).reshape(1, W)
-    gains[0] = own_gain
 
     def short(ext, taps, rows):
         once = pltpu.roll(ext, 1, 0)
@@ -286,25 +308,28 @@
     g_load.wait()
     out = filtered(128)
     gated[SPLIT:, :] = (qs[SPLIT:, :] * out[SPLIT - 128 :]).astype(BF16)
+    for copy in mix_loads:
+        copy.wait()
+    mixed(SPLIT, 192)
     pl.semaphore_wait(barrier, N - 1 + n_seq - 1)
     halos = [
-        send(qkv.at[i, pl.ds(R, H), :], qkv.at[i, pl.ds(0, H), :], halo_s.at[i], halo_r.at[i], after)
+        remote(qkv.at[i, pl.ds(R, H), :], qkv.at[i, pl.ds(0, H), :], halo_s.at[i], halo_r.at[i], after)
         for i in range(3)
     ]
-    rim = send(mu.at[pl.ds(R, 128), :], mu.at[pl.ds(0, 128), :], halo_s.at[3], halo_r.at[3], after)
-    for copy in mix_loads:
-        copy.wait()
-    mixed(SPLIT, 192)
+    rim = remote(mu.at[pl.ds(R, 128), :], mu.at[pl.ds(0, 128), :], halo_s.at[3], halo_r.at[3], after)
+    hand_on(*halos, rim)
     advance(0, 0)
     mixed(192, R)
     advance(1, 0)
 
+    gain_load.wait()
+    gains[0] = gain[...].astype(F32).reshape(1, W)
     gain_sends = [
         send(gains.at[0], gains.at[s], gain_s.at[s - 1], gain_r.at[s - 1], chan_peers[s - 1])
         for s in range(1, N)
     ]
     res_load = load(res_in, res_v)
-    more_loads = [load(f512_in, f512), load(g512_in, g512)]
+    more_loads = [load(f512_in, f512), load(g512_in, g512), load(li_short_in, li_short), load(slots_in, slots)]
     li_loads = [
         load(liw_in.at[:, pl.ds(pl.multiple_of(flipped(chan, s) * W, W), W), :], lw.at[:, pl.ds(s * W, W), :])
         for s in range(N)
@@ -315,8 +340,7 @@
 
     advance(0, 1)
 
-    for copy in halos:
-        copy.wait_recv()
+    handed(*halos)
     fixed = []
     ext_row = lax.broadcasted_iota(jnp.int32, (2 * H, W), 0)
     outside = jnp.logical_and(first, ext_row < H)
@@ -330,7 +354,7 @@
     ahead = out[: SPLIT - 128]
     ahead = ahead + jnp.where(lax.broadcasted_iota(jnp.int32, ahead.shape, 0) == 0, missed, 0.0)
     gated[128:SPLIT, :] = (qs[128:SPLIT, :] * ahead).astype(BF16)
-    rim.wait_recv()
+    handed(rim)
     mu[:128, :] = jnp.where(first, jnp.zeros((128, W), BF16), mu[:128, :])
     gated[:128, :] = (qs[:128, :] * filtered(0)).astype(BF16)
     mixed(0, 80)
@@ -378,13 +402,14 @@
 
     arrived(0, 1)
     project(SPLIT, R, row_scale(SPLIT, R), (0, 1, 2))
-    li_halo = send(lp.at[:, pl.ds(R, H), :], lp.at[:, pl.ds(0, H), :], halo_s.at[4], halo_r.at[4], after)
+    li_halo = remote(lp.at[:, pl.ds(R, H), :], lp.at[:, pl.ds(0, H), :], halo_s.at[4], halo_r.at[4], after)
+    hand_on(li_halo)
     li_inputs(160, R)
     li_queries(160, R)
     arrived(2, 3)
     inverse = row_scale(0, SPLIT)
     project(0, SPLIT, inverse, (1, 2))
-    li_halo.wait_recv()
+    handed(li_halo)
     li_inputs(0, 160)
     sb[...] = st[...].astype(BF16)
     states = [send(sb, sr.at[k + 1], st_s.at[k], st_r.at[k], seq_peers[k]) for k in range(n_seq - 1)]
@@ -447,6 +472,7 @@
     m_lane = lax.broadcasted_iota(jnp.int32, (MODES, W), 1) % MODES
     dec_out[...] = jnp.sum(jnp.where(m_row == m_lane, chosen, 0.0), axis=0, keepdims=True)
 
+    handed_on(*halos, rim, li_halo)
     for copy in pending:
         copy.wait_send()
     for copy in stores:
@@ -473,7 +499,6 @@
     tables = [jnp.asarray(a.astype(np.float32).astype(ml_dtypes.bfloat16)) for a in (f256, g256, f512, g512)]
     hbm = pl.BlockSpec(memory_space=pltpu.HBM)
     vmem = pl.BlockSpec(memory_space=pltpu.VMEM)
-    smem = pl.BlockSpec(memory_space=pltpu.SMEM)
     v = pltpu.VMEM
     dma = pltpu.SemaphoreType.DMA
     shapes = (
@@ -484,7 +509,7 @@
     done = pl.pallas_call(
         functools.partial(kernel, n_seq),
         out_shape=shapes,
-        in_specs=[hbm] * 13 + [vmem] * 3 + [smem],
+        in_specs=[hbm] * 17,
         out_specs=(hbm, hbm, vmem),
         scratch_shapes=[
             v((3, H + R, W), BF16),
@@ -522,7 +547,11 @@
             v((256, 512), BF16),
             v((MODES, W), F32),
             v((MODES, W), F32),
-            dma((30,)),
+            v((3, 3, W), BF16),
+            v((3, 3, W), BF16),
+            v((W,), BF16),
+            pltpu.SMEM((16,), jnp.int32),
+            dma((31,)),
             dma((5,)), dma((5,)),
             dma((len(PIECES), 3)), dma((len(PIECES), 3)),
             dma((len(PIECES), 2)), dma((len(PIECES), 2)),

time: 54.9 us -> 53.7 us (0.978)
  Pallas kernels: 54.1 us -> 52.9 us
    pallas_call x1, Pallas kernels: 52.3 us -> 51.1 us  [local(): pl.pallas_call(functools.partial(kernel, n_seq), out_shape=shapes, in_spe...]
where the time goes in v3:
time: 53.7 us; the launch traced here: 53.6 us
  Pallas kernels  52.9 us (99%)
  between operations  0.64 us (1%)
    pallas_call x1, Pallas kernels, local(): pl.pallas_call(functools.partial(kernel, n_seq), out_shape=shapes, in_spe...  51.1 us
    pallas_call x1, Pallas kernels, local(): pl.pallas_call(hand_over, out_shape=shapes, in_specs=[hbm] * 3, out_specs...  1.79 us

profile of v3, /device:TPU:1, one launch (start us, length us, event | category | flops | bytes accessed | tf_op | source)
XLA Modules:
  0.0 53.6 jit_solution(1822241356593702139)
XLA Ops:
  0.6 51.1 %layers.1 = (bf16[256,512]{1,0:T(8,128)(2,1)}, bf16[256,512]{1,0:T(8,128)(2,1)}, f32[1,512]{1,0:T(1,128)}) custom-call(bf16[256,512]{1,0:T(8,128)(2,1)} %res_in.1, bf16[256,512]{1,0:T(8,128)(2,1)} %q_in.1, bf16[256,512]{1,0:T(8,128)(2,1)} %k_in.1, bf16[256,512]{1,0:T(8,128)(2,1)} %v_in.1, bf16[512,4096]{1,0:T(8,128)(2,1)} %mix_in.1, ...), custom_call_target="tpu_custom_call" | custom-call | tf_op jit(solution)/shard_map/layers/pallas_call | solution.py:509
  51.8 1.8 %hand_over.1 = (bf16[256,512]{1,0:T(8,128)(2,1)}, bf16[256,512]{1,0:T(8,128)(2,1)}, f32[1,512]{1,0:T(1,128)}) custom-call(bf16[256,512]{1,0:T(8,128)(2,1)} %get-tuple-element.6.li_in, bf16[256,512]{1,0:T(8,128)(2,1)} %get-tuple-element.7.res_in, f32[1,512]{1,0:T(1,128)} %get-tuple-element.8.dec_in), custom_call_target="tpu_custom_call" | custom-call | tf_op jit(solution)/shard_map/hand_over/pallas_call | solution.py:570

commit v4 on v3

--- a/solution.py
+++ b/solution.py
@@ -81,7 +81,7 @@
     mr_short_in, li_short_in, gain_in, slots_in,
     li_out, res_out, dec_out,
     qkv, mu, qs, ht, gated, mw, part, rb1, rb2, rb3, res_v, hb, gains, inv_gains,
-    lw, lp, ql, ub, table, back, kern, lt, conv, st, sb, sr, lo_v, ro_v,
+    lw, lp, ql, ub, table, back, kern, lt, conv, st, sb, sr, choose, lo_v, ro_v,
     mr_filter, f256, g256, f512, g512, rate, residue, mr_short, li_short, gain, slots,
     load_sem, halo_s, halo_r, rs_s, rs_r, ag_s, ag_r, gain_s, gain_r, st_s, st_r, out_sem,
 ):
@@ -382,7 +382,6 @@
     advance(0, 4)
     for copy in more_loads:
         copy.wait()
-    kernel_spectrum()
     advance(2, 3)
     advance(3, 3)
     advance(1, 4)
@@ -401,11 +400,16 @@
                 flying[g, 4].wait_recv()
 
     arrived(0, 1)
-    project(SPLIT, R, row_scale(SPLIT, R), (0, 1, 2))
-    li_halo = remote(lp.at[:, pl.ds(R, H), :], lp.at[:, pl.ds(0, H), :], halo_s.at[4], halo_r.at[4], after)
+    inverse = row_scale(SPLIT, R)
+    last, border = pl.ds(R, H), pl.ds(0, H)
+    both = pl.ds(1, 2)
+    li_halo = remote(lp.at[both, last, :], lp.at[both, border, :], halo_s.at[4], halo_r.at[4], after)
+    query_halo = remote(lp.at[0, last, :], lp.at[0, border, :], halo_s.at[5], halo_r.at[5], after)
+    project(SPLIT, R, inverse, (1, 2))
     hand_on(li_halo)
     li_inputs(160, R)
-    li_queries(160, R)
+    project(SPLIT, R, inverse, (0,))
+    hand_on(query_halo)
     arrived(2, 3)
     inverse = row_scale(0, SPLIT)
     project(0, SPLIT, inverse, (1, 2))
@@ -414,8 +418,11 @@
     sb[...] = st[...].astype(BF16)
     states = [send(sb, sr.at[k + 1], st_s.at[k], st_r.at[k], seq_peers[k]) for k in range(n_seq - 1)]
     project(0, SPLIT, inverse, (0,))
+    li_queries(160, R)
+    handed(query_halo)
     li_queries(0, 160)
 
+    kernel_spectrum()
     x = jnp.dot(f512[...], ub[...], preferred_element_type=F32)
     xr, xi = x[:256], x[256:]
     y = jnp.concatenate(
@@ -427,6 +434,14 @@
     )
     conv[...] = jnp.dot(g512[...], y, preferred_element_type=F32)
 
+    mine = seq * N + chan
+    block = jnp.int32(0)
+    for b in range(slots.shape[0]):
+        block = block + jnp.where(slots[b] == mine, jnp.int32(b), jnp.int32(0))
+    source = lax.broadcasted_iota(jnp.int32, (W, W), 0) - block * CB
+    target = lax.broadcasted_iota(jnp.int32, (W, W), 1) // MODES
+    choose[...] = jnp.where(source == target, 1.0, 0.0).astype(BF16)
+
     sr[0] = sb[...]
     decay = jnp.exp(-rate[...] * float(R))
     leaving = residue[...] * jnp.exp(-rate[...])
@@ -458,21 +473,14 @@
     final = final * residue[...]
     high = final.astype(BF16)
     low = (final - high.astype(F32)).astype(BF16)
-    mine = seq * N + chan
-    block = jnp.int32(0)
-    for b in range(slots.shape[0]):
-        block = block + jnp.where(slots[b] == mine, jnp.int32(b), jnp.int32(0))
-    source = lax.broadcasted_iota(jnp.int32, (W, W), 0) - block * CB
-    target = lax.broadcasted_iota(jnp.int32, (W, W), 1) // MODES
-    choose = jnp.where(source == target, 1.0, 0.0).astype(BF16)
-    chosen = jnp.dot(high, choose, preferred_element_type=F32) + jnp.dot(
-        low, choose, preferred_element_type=F32
+    chosen = jnp.dot(high, choose[...], preferred_element_type=F32) + jnp.dot(
+        low, choose[...], preferred_element_type=F32
     )
     m_row = lax.broadcasted_iota(jnp.int32, (MODES, W), 0)
     m_lane = lax.broadcasted_iota(jnp.int32, (MODES, W), 1) % MODES
     dec_out[...] = jnp.sum(jnp.where(m_row == m_lane, chosen, 0.0), axis=0, keepdims=True)
 
-    handed_on(*halos, rim, li_halo)
+    handed_on(*halos, rim, li_halo, query_halo)
     for copy in pending:
         copy.wait_send()
     for copy in stores:
@@ -538,6 +546,7 @@
             v((MODES, W), F32),
             v((MODES, W), BF16),
             v((n_seq, MODES, W), BF16),
+            v((W, W), BF16),
             v((R, W), BF16),
             v((R, W), BF16),
             v((128, W), BF16),
@@ -552,7 +561,7 @@
             v((W,), BF16),
             pltpu.SMEM((16,), jnp.int32),
             dma((31,)),
-            dma((5,)), dma((5,)),
+            dma((6,)), dma((6,)),
             dma((len(PIECES), 3)), dma((len(PIECES), 3)),
             dma((len(PIECES), 2)), dma((len(PIECES), 2)),
             dma((N - 1,)), dma((N - 1,)),

time: 53.7 us -> 53.4 us (level)
  no operation moved by 1% of the time
where the time goes in v4:
time: 53.4 us; the launch traced here: 53.2 us
  Pallas kernels  52.6 us (99%)
  between operations  0.64 us (1%)
    pallas_call x1, Pallas kernels, local(): pl.pallas_call(functools.partial(kernel, n_seq), out_shape=shapes, in_spe...  50.8 us
    pallas_call x1, Pallas kernels, local(): pl.pallas_call(hand_over, out_shape=shapes, in_specs=[hbm] * 3, out_specs...  1.79 us

profile of v4, /device:TPU:1, one launch (start us, length us, event | category | flops | bytes accessed | tf_op | source)
XLA Modules:
  0.0 53.2 jit_solution(4024559486319619537)
XLA Ops:
  0.6 50.8 %layers.1 = (bf16[256,512]{1,0:T(8,128)(2,1)}, bf16[256,512]{1,0:T(8,128)(2,1)}, f32[1,512]{1,0:T(1,128)}) custom-call(bf16[256,512]{1,0:T(8,128)(2,1)} %res_in.1, bf16[256,512]{1,0:T(8,128)(2,1)} %q_in.1, bf16[256,512]{1,0:T(8,128)(2,1)} %k_in.1, bf16[256,512]{1,0:T(8,128)(2,1)} %v_in.1, bf16[512,4096]{1,0:T(8,128)(2,1)} %mix_in.1, ...), custom_call_target="tpu_custom_call" | custom-call | tf_op jit(solution)/shard_map/layers/pallas_call | solution.py:517
  51.4 1.8 %hand_over.1 = (bf16[256,512]{1,0:T(8,128)(2,1)}, bf16[256,512]{1,0:T(8,128)(2,1)}, f32[1,512]{1,0:T(1,128)}) custom-call(bf16[256,512]{1,0:T(8,128)(2,1)} %get-tuple-element.6.li_in, bf16[256,512]{1,0:T(8,128)(2,1)} %get-tuple-element.7.res_in, f32[1,512]{1,0:T(1,128)} %get-tuple-element.8.dec_in), custom_call_target="tpu_custom_call" | custom-call | tf_op jit(solution)/shard_map/hand_over/pallas_call | solution.py:579

commit v5 on v4

--- a/solution.py
+++ b/solution.py
@@ -81,7 +81,7 @@
     mr_short_in, li_short_in, gain_in, slots_in,
     li_out, res_out, dec_out,
     qkv, mu, qs, ht, gated, mw, part, rb1, rb2, rb3, res_v, hb, gains, inv_gains,
-    lw, lp, ql, ub, table, back, kern, lt, conv, st, sb, sr, choose, lo_v, ro_v,
+    lw, lp, ql, ub, table, back, kern, lt, conv, st, sb, sr, choose, lo_v, ro_v, dec_v,
     mr_filter, f256, g256, f512, g512, rate, residue, mr_short, li_short, gain, slots,
     load_sem, halo_s, halo_r, rs_s, rs_r, ag_s, ag_r, gain_s, gain_r, st_s, st_r, out_sem,
 ):
@@ -478,7 +478,9 @@
     )
     m_row = lax.broadcasted_iota(jnp.int32, (MODES, W), 0)
     m_lane = lax.broadcasted_iota(jnp.int32, (MODES, W), 1) % MODES
-    dec_out[...] = jnp.sum(jnp.where(m_row == m_lane, chosen, 0.0), axis=0, keepdims=True)
+    dec_v[...] = jnp.sum(jnp.where(m_row == m_lane, chosen, 0.0), axis=0, keepdims=True)
+    stores.append(pltpu.make_async_copy(dec_v, dec_out, out_sem.at[3]))
+    stores[-1].start()
 
     handed_on(*halos, rim, li_halo, query_halo)
     for copy in pending:
@@ -518,7 +520,7 @@
         functools.partial(kernel, n_seq),
         out_shape=shapes,
         in_specs=[hbm] * 17,
-        out_specs=(hbm, hbm, vmem),
+        out_specs=(hbm, hbm, hbm),
         scratch_shapes=[
             v((3, H + R, W), BF16),
             v((128 + R, W), BF16),
@@ -549,6 +551,7 @@
             v((W, W), BF16),
             v((R, W), BF16),
             v((R, W), BF16),
+            v((1, CB * MODES), F32),
             v((128, W), BF16),
             v((256, 256), BF16),
             v((128, 256), BF16),
@@ -566,7 +569,7 @@
             dma((len(PIECES), 2)), dma((len(PIECES), 2)),
             dma((N - 1,)), dma((N - 1,)),
             dma((n_seq - 1,)), dma((n_seq - 1,)),
-            dma((3,)),
+            dma((4,)),
         ],
         compiler_params=pltpu.CompilerParams(
             collective_id=0, has_side_effects=True, vmem_limit_bytes=60 * 1024 * 1024

time: 53.4 us -> 53 us (level)
  no operation moved by 1% of the time
where the time goes in v5:
time: 53 us; the launch traced here: 52.8 us
  Pallas kernels  52.2 us (98%)
  between operations  0.64 us (1%)
    pallas_call x1, Pallas kernels, local(): pl.pallas_call(functools.partial(kernel, n_seq), out_shape=shapes, in_spe...  50.4 us
    pallas_call x1, Pallas kernels, local(): pl.pallas_call(hand_over, out_shape=shapes, in_specs=[hbm] * 3, out_specs...  1.79 us

profile of v5, /device:TPU:1, one launch (start us, length us, event | category | flops | bytes accessed | tf_op | source)
XLA Modules:
  0.0 52.8 jit_solution(16369716605988646159)
XLA Ops:
  0.6 50.4 %layers.1 = (bf16[256,512]{1,0:T(8,128)(2,1)}, bf16[256,512]{1,0:T(8,128)(2,1)}, f32[1,512]{1,0:T(1,128)}) custom-call(bf16[256,512]{1,0:T(8,128)(2,1)} %res_in.1, bf16[256,512]{1,0:T(8,128)(2,1)} %q_in.1, bf16[256,512]{1,0:T(8,128)(2,1)} %k_in.1, bf16[256,512]{1,0:T(8,128)(2,1)} %v_in.1, bf16[512,4096]{1,0:T(8,128)(2,1)} %mix_in.1, ...), custom_call_target="tpu_custom_call" | custom-call | tf_op jit(solution)/shard_map/layers/pallas_call | solution.py:519
  51.0 1.8 %hand_over.1 = (bf16[256,512]{1,0:T(8,128)(2,1)}, bf16[256,512]{1,0:T(8,128)(2,1)}, f32[1,512]{1,0:T(1,128)}) custom-call(bf16[256,512]{1,0:T(8,128)(2,1)} %get-tuple-element.6.li_in, bf16[256,512]{1,0:T(8,128)(2,1)} %get-tuple-element.7.res_in, f32[1,512]{1,0:T(1,128)} %get-tuple-element.8.dec_in), custom_call_target="tpu_custom_call" | custom-call | tf_op jit(solution)/shard_map/hand_over/pallas_call | solution.py:582
